TPU v7x, 32 devices: a whole 2x2x4 slice. The times are simulated.
32 devices in a mesh: dp: 4 (over y, x), ctx: 8 (over z, core).
Axes of the slice: x: 2, y: 2, z: 4, core: 2. Of those that a mesh axis runs over, the one named last changes fastest.
Arguments:
- queries: bfloat16 [8192, 4096], P(('dp', 'ctx')), may hold values from -5 to 5
- conv_keys: bfloat16 [8192, 512], P(('dp', 'ctx')), may hold values from -5 to 5
- conv_values: bfloat16 [8192, 512], P(('dp', 'ctx')), may hold values from -5 to 5
- out_grad: bfloat16 [8192, 4096], P(('dp', 'ctx')), may hold values from -5 to 5
- segment_ids: int32 [32, 256], P(('dp', 'ctx')), may hold values from 0 to 2, never falling along the last dimension, each value on 1 to 128 neighbouring positions
- cart_keys: bfloat16 [256, 512], P('ctx'), may hold values from -5 to 5
- cart_values: bfloat16 [256, 512], P('ctx'), may hold values from -5 to 5
Outputs:
- cart_key_grad: float32 [256, 512], P('ctx')
- cart_value_grad: float32 [256, 512], P('ctx')
Inputs may be any that keep to these rules, and one draw needn't show every extreme that they name: `segment_ids`: within a block the numbers never fall; each block holds 3 conversations of 1 to 128 tokens, one of exactly 128.
All inputs are finite; a program needn't handle non-finite values.
Results may differ from a plain program's by a relative error of at most 0.0041.
Values may be sent and summed in bfloat16 or wider, within the bound.
A program may use at most 128 MiB of HBM per device.

v0:
```python
import math

import jax
import jax.numpy as jnp
from jax import lax
from jax.sharding import PartitionSpec as P

HD = 128


def split_heads(array, heads):
    return jnp.moveaxis(array.reshape(array.shape[0], heads, HD), 1, 0)


def group_stats(items, allowed, scale):
    query_group, cart_key, cart_value, conv_key, conv_value = items
    score_cart = (
        jnp.einsum("tgd,jd->tgj", query_group, cart_key, preferred_element_type=jnp.float32) * scale
    )
    score_conv = (
        jnp.einsum("tgd,ud->tgu", query_group, conv_key, preferred_element_type=jnp.float32) * scale
    )
    score_conv = jnp.where(allowed[:, None, :], score_conv, -jnp.inf)
    top = jnp.maximum(jnp.max(score_cart, axis=-1), jnp.max(score_conv, axis=-1))
    exp_cart = jnp.exp(score_cart - top[..., None])
    exp_conv = jnp.exp(score_conv - top[..., None])
    total = jnp.sum(exp_cart, axis=-1) + jnp.sum(exp_conv, axis=-1)
    probs_cart = (exp_cart / total[..., None]).astype(jnp.bfloat16)
    probs_conv = (exp_conv / total[..., None]).astype(jnp.bfloat16)
    mixed = jnp.einsum("tgj,jd->tgd", probs_cart, cart_value, preferred_element_type=jnp.float32)
    mixed = mixed + jnp.einsum(
        "tgu,ud->tgd", probs_conv, conv_value, preferred_element_type=jnp.float32
    )
    return (top, total, mixed)


def group_grads(items, scale):
    query_group, grad_group, top, total, delta, key_rows, value_rows = items
    score = (
        jnp.einsum("tgd,jd->tgj", query_group, key_rows, preferred_element_type=jnp.float32) * scale
    )
    probs = jnp.exp(score - top[..., None]) / total[..., None]
    probs_b = probs.astype(jnp.bfloat16)
    dprob = jnp.einsum("tgd,jd->tgj", grad_group, value_rows, preferred_element_type=jnp.float32)
    dscore_b = (probs * (dprob - delta[..., None])).astype(jnp.bfloat16)
    value_grad = jnp.einsum("tgj,tgd->jd", probs_b, grad_group, preferred_element_type=jnp.float32)
    key_grad = (
        jnp.einsum("tgj,tgd->jd", dscore_b, query_group, preferred_element_type=jnp.float32) * scale
    )
    return (key_grad, value_grad)


def per_device(queries, conv_keys, conv_values, out_grad, segment_ids, cart_keys, cart_values):
    scale = 1.0 / math.sqrt(HD)
    kv_heads = cart_keys.shape[1] // HD
    group = queries.shape[1] // (kv_heads * HD)
    tokens = queries.shape[0]
    full_keys, full_values = (
        lax.all_gather(cart_keys, "ctx", axis=0, tiled=True),
        lax.all_gather(cart_values, "ctx", axis=0, tiled=True),
    )
    segments = segment_ids[0]
    position = jnp.arange(tokens)
    allowed = (segments[:, None] == segments[None, :]) & (position[None, :] <= position[:, None])
    query_heads = jnp.moveaxis(queries.reshape(tokens, kv_heads, group, HD), 1, 0)
    grad_heads = jnp.moveaxis(out_grad.reshape(tokens, kv_heads, group, HD), 1, 0)
    conv_key_heads = split_heads(conv_keys, kv_heads)
    conv_value_heads = split_heads(conv_values, kv_heads)
    tops, totals, mixed = lax.map(
        lambda items: group_stats(items, allowed, scale),
        (
            query_heads,
            split_heads(full_keys, kv_heads),
            split_heads(full_values, kv_heads),
            conv_key_heads,
            conv_value_heads,
        ),
    )
    deltas = jnp.sum(grad_heads.astype(jnp.float32) * mixed, axis=-1)
    count = full_keys.shape[0]
    key_grads, value_grads = lax.map(
        lambda items: group_grads(items, scale),
        (
            query_heads,
            grad_heads,
            tops,
            totals,
            deltas,
            split_heads(full_keys, kv_heads),
            split_heads(full_values, kv_heads),
        ),
    )
    key_part = jnp.moveaxis(key_grads, 0, 1).reshape(count, kv_heads * HD)
    value_part = jnp.moveaxis(value_grads, 0, 1).reshape(count, kv_heads * HD)
    partial_sum = lax.psum_scatter(
        jnp.concatenate([key_part, value_part], axis=1), "ctx", scatter_dimension=0, tiled=True
    )
    summed = lax.psum(partial_sum, "dp")
    return (summed[:, : kv_heads * HD], summed[:, kv_heads * HD :])


def solution(mesh):
    in_specs = (
        P(("dp", "ctx"), None),
        P(("dp", "ctx"), None),
        P(("dp", "ctx"), None),
        P(("dp", "ctx"), None),
        P(("dp", "ctx"), None),
        P("ctx", None),
        P("ctx", None),
    )
    out_specs = (P("ctx", None), P("ctx", None))
    return jax.shard_map(
        per_device, mesh=mesh, in_specs=in_specs, out_specs=out_specs, check_vma=False
    )
```

profile of v0, /device:TPU:0, one launch (start us, length us, event | category | flops | bytes accessed | tf_op | source)
XLA Modules:
  0.0 197.2 jit_solution(16874385741344055014)
XLA Ops:
  7.3 3.3 %copy.41 = bf16[256,4096]{0,1:T(8,128)(2,1)S(1)} copy(bf16[256,4096]{1,0:T(8,128)(2,1)} %param.11) | data formatting | bytes 4194304 | tf_op args[0]
  10.6 2.4 %copy.53 = bf16[4,256,8,128]{3,1,2,0:T(8,128)(2,1)} copy(bf16[4,256,8,128]{1,3,2,0:T(8,128)(2,1)S(1)} %bitcast.154) | data formatting | bytes 4194304 | tf_op jit(solution)/shard_map/while | solution.py:81
  13.0 16.0 %all_gather.7 = bf16[256,512]{1,0:T(8,128)(2,1)S(1)} all-gather(bf16[32,512]{1,0:T(8,128)(2,1)S(1)} %copy-done.3), channel_id=1, replica_groups=mesh['dp'=4,'ctx'=8] {'ctx'}, dimensions={0}, use_global_device_ids=true | all-gather | bytes 294912 | tf_op jit(solution)/shard_map/all_gather | solution.py:60
  29.0 0.1 copy.44
  29.1 0.2 copy.49
  29.3 14.2 %all_gather.6 = bf16[256,512]{1,0:T(8,128)(2,1)S(1)} all-gather(bf16[32,512]{1,0:T(8,128)(2,1)S(1)} %copy-done.4), channel_id=1, replica_groups=mesh['dp'=4,'ctx'=8] {'ctx'}, dimensions={0}, use_global_device_ids=true | all-gather | bytes 294912 | tf_op jit(solution)/shard_map/all_gather | solution.py:59
  43.5 0.1 copy.42
  43.7 0.2 copy.54
  43.8 0.1 copy.43
  44.0 0.9 copy.45
  44.9 31.2 %while.28 = (s32[]{:T(128)}, f32[4,256,8]{1,2,0:T(8,128)S(1)}, f32[4,256,8]{1,2,0:T(8,128)S(1)}, f32[4,256,8,128]{1,3,2,0:T(8,128)}, bf16[4,256,8,128]{3,1,2,0:T...) while((s32[]{:T(128)}, f32[4,256,8]{1,2,0:T(8,128)S(1)}, ...), condition=%wide.region_5.6_spmd.clone, body=%wide.region_0.5_spmd.clone.sunk | while | flops 548335616 | bytes 21639288 | solution.py:69
  44.9 0.1 fusion.91
  45.0 1.5 fusion.92
  46.5 1.5 multiply_reduce_fusion.3
  48.0 0.8 fusion.93
  48.8 0.7 fusion.94
  49.5 1.7 fusion.95
  51.2 0.3 copy.74
  51.5 1.1 constant_dynamic-update-slice_fusion.2
  52.7 0.1 fusion.91
  52.8 1.5 fusion.92
  54.3 1.5 multiply_reduce_fusion.3
  55.8 0.8 fusion.93
  56.6 0.7 fusion.94
  57.3 1.7 fusion.95
  59.0 0.3 copy.74
  59.3 1.1 constant_dynamic-update-slice_fusion.2
  60.5 0.1 fusion.91
  60.6 1.5 fusion.92
  62.1 1.5 multiply_reduce_fusion.3
  63.7 0.8 fusion.93
  64.5 0.7 fusion.94
  65.1 1.7 fusion.95
  66.8 0.3 copy.74
  67.2 1.1 constant_dynamic-update-slice_fusion.2
  68.3 0.1 fusion.91
  68.4 1.5 fusion.92
  70.0 1.5 multiply_reduce_fusion.3
  71.5 0.8 fusion.93
  72.3 0.7 fusion.94
  72.9 1.7 fusion.95
  74.7 0.3 copy.74
  75.0 1.1 constant_dynamic-update-slice_fusion.2
  76.1 4.1 %copy.51 = bf16[256,4096]{0,1:T(8,128)(2,1)} copy(bf16[256,4096]{1,0:T(8,128)(2,1)} %param.14) | data formatting | bytes 4194304 | tf_op args[3]
  80.2 3.6 %multiply_reduce_fusion.1 = f32[4,256,8]{1,2,0:T(8,128)S(1)} fusion(f32[4,256,8,128]{1,3,2,0:T(8,128)} %get-tuple-element.111, bf16[256,4096]{0,1:T(8,128)(2,1)} %copy.51), kind=kLoop, calls=%fused_computation.72 | loop fusion | flops 3137536 | bytes 6324224 | tf_op jit(solution)/shard_map/reduce_sum | solution.py:79
  83.7 26.0 %while.27 = (s32[]{:T(128)}, f32[4,256,128]{2,1,0:T(8,128)S(1)}, f32[4,256,128]{2,1,0:T(8,128)}, bf16[4,256,8,128]{3,1,2,0:T(8,128)(2,1)}, bf16[4,256,128]{2,1,0...) while((s32[]{:T(128)}, f32[4,256,128]{2,1,0:T(8,128)S(1)}, ...), condition=%wide.region_8.9_spmd, body=%wide.region_7.8_spmd.sunk | while | flops 540573696 | bytes 8859765 | solution.py:81
  83.8 1.8 exponential_divide_fusion.2
  85.6 2.2 %fusion.88 = f32[4,256,128]{2,1,0:T(8,128)} fusion(f32[4,256,128]{2,1,0:T(8,128)} %get-tuple-element.425, s32[]{:T(128)} %get-tuple-element.423, f32[256,8,256]{2,0,1:T(8,128)S(1)} %exponential_divide_fusion.2, bf16[4,256,8,128]{1,3,2,0:T(8,128)(2,1)} %get-tuple-element.441), kind=kOutput, calls=%fused_computation.6.clone.1 | convolution fusion | flops 134742016 | bytes 2753536 | tf_op jit(solution)/shard_map/while/body/eval_jaxpr/tgj,tgd->jd/dot_general | solution.py:46
  87.8 2.4 %fusion.87 = f32[4,256,128]{2,1,0:T(8,128)S(1)} fusion(f32[4,256,128]{2,1,0:T(8,128)S(1)} %get-tuple-element.424, s32[]{:T(128)} %get-tuple-element.423, f32[256,8,256]{2,0,1:T(8,128)S(1)} %exponential_divide_fusion.2, f32[256,8]{0,1:T(8,128)S(1)} %get-tuple-element.358, bf16[4,256,8,128]{1,3,2,0:T(8,128)(2,1)} %get-tuple-element.441, ...), kind=kOutput, calls=%fused_computation.9.clone.1 | convolution fusion | flops 270041088 | bytes 3352576 | tf_op jit(solution)/shard_map/while/body/eval_jaxpr/tgj,tgd->jd/dot_general | solution.py:48
  90.3 1.8 exponential_divide_fusion.2
  92.1 2.2 %fusion.88 = f32[4,256,128]{2,1,0:T(8,128)} fusion(f32[4,256,128]{2,1,0:T(8,128)} %get-tuple-element.425, s32[]{:T(128)} %get-tuple-element.423, f32[256,8,256]{2,0,1:T(8,128)S(1)} %exponential_divide_fusion.2, bf16[4,256,8,128]{1,3,2,0:T(8,128)(2,1)} %get-tuple-element.441), kind=kOutput, calls=%fused_computation.6.clone.1 | convolution fusion | flops 134742016 | bytes 2753536 | tf_op jit(solution)/shard_map/while/body/eval_jaxpr/tgj,tgd->jd/dot_general | solution.py:46
  94.3 2.4 %fusion.87 = f32[4,256,128]{2,1,0:T(8,128)S(1)} fusion(f32[4,256,128]{2,1,0:T(8,128)S(1)} %get-tuple-element.424, s32[]{:T(128)} %get-tuple-element.423, f32[256,8,256]{2,0,1:T(8,128)S(1)} %exponential_divide_fusion.2, f32[256,8]{0,1:T(8,128)S(1)} %get-tuple-element.358, bf16[4,256,8,128]{1,3,2,0:T(8,128)(2,1)} %get-tuple-element.441, ...), kind=kOutput, calls=%fused_computation.9.clone.1 | convolution fusion | flops 270041088 | bytes 3352576 | tf_op jit(solution)/shard_map/while/body/eval_jaxpr/tgj,tgd->jd/dot_general | solution.py:48
  96.8 1.8 exponential_divide_fusion.2
  98.6 2.2 %fusion.88 = f32[4,256,128]{2,1,0:T(8,128)} fusion(f32[4,256,128]{2,1,0:T(8,128)} %get-tuple-element.425, s32[]{:T(128)} %get-tuple-element.423, f32[256,8,256]{2,0,1:T(8,128)S(1)} %exponential_divide_fusion.2, bf16[4,256,8,128]{1,3,2,0:T(8,128)(2,1)} %get-tuple-element.441), kind=kOutput, calls=%fused_computation.6.clone.1 | convolution fusion | flops 134742016 | bytes 2753536 | tf_op jit(solution)/shard_map/while/body/eval_jaxpr/tgj,tgd->jd/dot_general | solution.py:46
  100.8 2.4 %fusion.87 = f32[4,256,128]{2,1,0:T(8,128)S(1)} fusion(f32[4,256,128]{2,1,0:T(8,128)S(1)} %get-tuple-element.424, s32[]{:T(128)} %get-tuple-element.423, f32[256,8,256]{2,0,1:T(8,128)S(1)} %exponential_divide_fusion.2, f32[256,8]{0,1:T(8,128)S(1)} %get-tuple-element.358, bf16[4,256,8,128]{1,3,2,0:T(8,128)(2,1)} %get-tuple-element.441, ...), kind=kOutput, calls=%fused_computation.9.clone.1 | convolution fusion | flops 270041088 | bytes 3352576 | tf_op jit(solution)/shard_map/while/body/eval_jaxpr/tgj,tgd->jd/dot_general | solution.py:48
  103.3 1.8 exponential_divide_fusion.2
  105.1 2.2 %fusion.88 = f32[4,256,128]{2,1,0:T(8,128)} fusion(f32[4,256,128]{2,1,0:T(8,128)} %get-tuple-element.425, s32[]{:T(128)} %get-tuple-element.423, f32[256,8,256]{2,0,1:T(8,128)S(1)} %exponential_divide_fusion.2, bf16[4,256,8,128]{1,3,2,0:T(8,128)(2,1)} %get-tuple-element.441), kind=kOutput, calls=%fused_computation.6.clone.1 | convolution fusion | flops 134742016 | bytes 2753536 | tf_op jit(solution)/shard_map/while/body/eval_jaxpr/tgj,tgd->jd/dot_general | solution.py:46
  107.3 2.4 %fusion.87 = f32[4,256,128]{2,1,0:T(8,128)S(1)} fusion(f32[4,256,128]{2,1,0:T(8,128)S(1)} %get-tuple-element.424, s32[]{:T(128)} %get-tuple-element.423, f32[256,8,256]{2,0,1:T(8,128)S(1)} %exponential_divide_fusion.2, f32[256,8]{0,1:T(8,128)S(1)} %get-tuple-element.358, bf16[4,256,8,128]{1,3,2,0:T(8,128)(2,1)} %get-tuple-element.441, ...), kind=kOutput, calls=%fused_computation.9.clone.1 | convolution fusion | flops 270041088 | bytes 3352576 | tf_op jit(solution)/shard_map/while/body/eval_jaxpr/tgj,tgd->jd/dot_general | solution.py:48
  109.7 1.2 copy_bitcast_fusion
  110.9 1.1 pad_maximum_fusion
  112.0 0.0 all-reduce.2.cloned.1.call-start
  112.1 33.5 %reduce-scatter.2.cloned.1.call-done = f32[32,1024]{1,0:T(8,128)} async-done(((f32[256,1024]{1,0:T(8,128)}), f32[32,1024]{1,0:T(8,128)}) %reduce-scatter.2.cloned.1.call-update) | async-done | bytes 131088 | tf_op jit(solution)/shard_map/reduce_scatter | solution.py:95
  145.6 43.2 %all-reduce.2.cloned.1.call-done = f32[32,1024]{1,0:T(8,128)} async-done(((f32[32,1024]{1,0:T(8,128)}), f32[32,1024]{1,0:T(8,128)}) %all-reduce.2.cloned.1.call-update) | async-done | bytes 131088 | tf_op jit(solution)/shard_map/psum | solution.py:98
  188.9 1.5 fusion.61
  (34 shorter events, 0.2 us)
Async XLA Ops:
  7.2 138.4 %reduce-scatter.2.cloned.1.call-start = ((), (), s32[]{:S(2)}) async-start(), calls=%async_computation.1 | async-start | bytes 1179648 | tf_op jit(solution)/shard_map/reduce_scatter | solution.py:95
  10.5 2.4 %copy-start.3 = (bf16[32,512]{1,0:T(8,128)(2,1)S(1)}, bf16[32,512]{1,0:T(8,128)(2,1)}, u32[]{:S(2)}) copy-start(bf16[32,512]{1,0:T(8,128)(2,1)} %param.17) | copy-start | bytes 98308
  10.6 18.8 %copy-start.4 = (bf16[32,512]{1,0:T(8,128)(2,1)S(1)}, bf16[32,512]{1,0:T(8,128)(2,1)}, u32[]{:S(2)}) copy-start(bf16[32,512]{1,0:T(8,128)(2,1)} %param.16) | copy-start | bytes 98308
  13.0 30.9 %copy-start = (bf16[256,512]{1,0:T(8,128)(2,1)S(1)}, bf16[256,512]{1,0:T(8,128)(2,1)}, u32[]{:S(2)}) copy-start(bf16[256,512]{1,0:T(8,128)(2,1)} %param.12) | copy-start | bytes 786436
  13.0 31.0 %copy-start.1 = (bf16[256,512]{1,0:T(8,128)(2,1)S(1)}, bf16[256,512]{1,0:T(8,128)(2,1)}, u32[]{:S(2)}) copy-start(bf16[256,512]{1,0:T(8,128)(2,1)} %param.13) | copy-start | bytes 786436
  13.0 31.9 %copy-start.2 = (s32[1,256]{1,0:T(1,128)S(1)}, s32[1,256]{1,0:T(1,128)}, u32[]{:S(2)}) copy-start(s32[1,256]{1,0:T(1,128)} %param.15) | copy-start | bytes 3076
  112.0 76.9 %all-reduce.2.cloned.1.call-start = ((), (), s32[]{:S(2)}) async-start(), calls=%async_computation.2 | async-start | bytes 262144 | tf_op jit(solution)/shard_map/psum | solution.py:98
Sparse Core Ops, SparseCore 0:
  112.1 33.4 reduce-scatter.1
  148.5 40.3 all-reduce.1
where the time goes:
time: 199 us; the launch traced here: 197 us
  waiting for transfers between devices  76.8 us (39%)
  matrix products  47.3 us (24%)
  blocking collectives  30.2 us (15%)
  local copies, waits for them, and re-layouts  20 us (10%)
  between operations  14.2 us (7%)
  other arithmetic  8.29 us (4%)
    psum x1, waiting for transfers between devices, per_device(): summed = lax.psum(partial_sum, 'dp')  43.2 us
    reduce_scatter x1, waiting for transfers between devices, per_device(): lax.psum_scatter(jnp.concatenate([key_part, value_part], axis=1), 'ctx',...  33.5 us
    all_gather x1, blocking collectives, per_device(): lax.all_gather(cart_values, 'ctx', axis=0, tiled=True)  16 us
    all_gather x1, blocking collectives, per_device(): lax.all_gather(cart_keys, 'ctx', axis=0, tiled=True)  14.2 us
    dot_general x4, matrix products, group_grads(): jnp.einsum('tgj,tgd->jd', dscore_b, query_group, preferred_element_type=j...  9.64 us
    dot_general x4, matrix products, group_grads(): jnp.einsum('tgj,tgd->jd', probs_b, grad_group, preferred_element_type=jnp...  8.73 us
    unnamed x15, local copies, waits for them, and re-layouts  8.55 us
    dot_general x4, matrix products, group_grads(): jnp.einsum('tgd,jd->tgj', query_group, key_rows, preferred_element_type=j...  7.34 us
  transfers between devices with their start and end apart: 2, of which 2 were waited for; matrix products, arithmetic and copies ran while one was open for 0% of the time, Pallas kernels for 0%

commit v1 on v0

v1 whole, which is shorter than its diff:
```python
import functools
import math

import jax
import jax.numpy as jnp
from jax import lax
from jax.experimental import pallas as pl
from jax.experimental.pallas import tpu as pltpu
from jax.sharding import PartitionSpec as P

HD = 128
MESH = pl.DeviceIdType.MESH
NT = (((1,), (1,)), ((), ()))


def dot_nt(a, b):
    return lax.dot_general(a, b, NT, preferred_element_type=jnp.float32)


def dot(a, b):
    return jnp.dot(a, b, preferred_element_type=jnp.float32)


def kernel(
    n, nd, groups, heads,
    q_hbm, ck_hbm, cv_hbm, og_hbm, seg_hbm, kk_hbm, kv_hbm,
    dk_ref, dv_ref,
    q_s, og_s, ck_s, cv_s, seg_s, bias, stats, buf, part, r1, s2, r2, r3,
    in_sem, conv_sem, cart_sem,
    g_send, g_recv, f_send, f_recv, s1_send, s1_recv, s2_send, s2_recv, s3_send, s3_recv,
):
    dp, me = lax.axis_index("dp"), lax.axis_index("ctx")
    half = n // 2
    core = lax.rem(me, 2)
    place = me // 2
    sibling = me + 1 - 2 * core
    tokens = q_s.shape[0]
    rows = buf.shape[2]
    cart = n * rows
    width = heads * HD
    scale = 1.0 / math.sqrt(HD)
    factor = scale * math.log2(math.e)

    barrier = pltpu.get_barrier_semaphore()
    pl.semaphore_signal(barrier, inc=1, device_id=(dp, sibling), device_id_type=MESH)
    for i in range(1, half):
        pl.semaphore_signal(
            barrier, inc=1, device_id=(dp, lax.rem(me + 2 * i, n)), device_id_type=MESH
        )
    for i in range(1, nd):
        pl.semaphore_signal(
            barrier, inc=1, device_id=(lax.rem(dp + i, nd), me), device_id_type=MESH
        )

    cart_copies = []
    for g in range(groups):
        cols = pl.ds(g * HD, HD)
        cart_copies.append(
            pltpu.make_async_copy(kk_hbm.at[:, cols], buf.at[me, g], cart_sem.at[g])
        )
        cart_copies.append(
            pltpu.make_async_copy(
                kv_hbm.at[:, cols], buf.at[me, groups + g], cart_sem.at[groups + g]
            )
        )
    for copy in cart_copies:
        copy.start()
    conv_copies = [
        pltpu.make_async_copy(seg_hbm, seg_s, conv_sem.at[0]),
        pltpu.make_async_copy(ck_hbm, ck_s, conv_sem.at[1]),
        pltpu.make_async_copy(cv_hbm, cv_s, conv_sem.at[2]),
    ]
    for copy in conv_copies:
        copy.start()
    in_copies = []
    for g in range(groups):
        cols = pl.ds(g * width, width)
        in_copies.append(
            (
                pltpu.make_async_copy(q_hbm.at[:, cols], q_s.at[:, cols], in_sem.at[0, g]),
                pltpu.make_async_copy(og_hbm.at[:, cols], og_s.at[:, cols], in_sem.at[1, g]),
            )
        )
        for copy in in_copies[-1]:
            copy.start()
    for copy in cart_copies:
        copy.wait()
    pl.semaphore_wait(barrier, 1 + (half - 1) + (nd - 1))

    def remote(src, dst, send, recv, target):
        return pltpu.make_async_remote_copy(
            src_ref=src, dst_ref=dst, send_sem=send, recv_sem=recv,
            device_id=target, device_id_type=MESH,
        )

    gather = [
        remote(
            buf.at[me], buf.at[me], g_send.at[i], g_recv.at[i], (dp, lax.rem(me + 2 * i, n))
        )
        for i in range(1, half)
    ]
    arrivals = [lax.rem(me + n - 2 * i, n) for i in range(half)]
    forward = [
        remote(buf.at[a], buf.at[a], f_send.at[i], f_recv.at[i], (dp, sibling))
        for i, a in enumerate(arrivals)
    ]
    for copy in gather:
        copy.start()
    forward[0].start()

    for copy in conv_copies:
        copy.wait()
    seg_row = jnp.broadcast_to(seg_s[...].astype(jnp.float32), (tokens, tokens))
    key_at = lax.broadcasted_iota(jnp.int32, (tokens, tokens), 0)
    token_at = lax.broadcasted_iota(jnp.int32, (tokens, tokens), 1)
    allowed = (seg_row == seg_row.T) & (key_at <= token_at)
    bias[...] = jnp.where(allowed, 0.0, -1e30)
    mid = tokens // 2

    def conv_head(g, j):
        cols = pl.ds(pl.multiple_of(g * width + j * HD, HD), HD)
        key = ck_s[:, g * HD : (g + 1) * HD]
        value = cv_s[:, g * HD : (g + 1) * HD]
        q, og = q_s[:, cols], og_s[:, cols]
        x0 = dot_nt(key[:mid], q) * factor + bias[:mid, :]
        x1 = dot_nt(key[mid:], q[mid:]) * factor + bias[mid:, mid:]
        d0 = dot_nt(value[:mid], og)
        d1 = dot_nt(value[mid:], og[mid:])
        top0 = jnp.max(x0, axis=0, keepdims=True)
        top1 = jnp.max(x1, axis=0, keepdims=True)
        top = jnp.concatenate([top0[:, :mid], jnp.maximum(top0[:, mid:], top1)], axis=1)
        e0 = jnp.exp2(x0 - top)
        e1 = jnp.exp2(x1 - top[:, mid:])
        l0 = jnp.sum(e0, axis=0, keepdims=True)
        l1 = jnp.sum(e1, axis=0, keepdims=True)
        a0 = jnp.sum(e0 * d0, axis=0, keepdims=True)
        a1 = jnp.sum(e1 * d1, axis=0, keepdims=True)
        h = g * heads + j
        stats[h, 0:1, :] = top
        stats[h, 1:2, :] = jnp.concatenate([l0[:, :mid], l0[:, mid:] + l1], axis=1)
        stats[h, 2:3, :] = jnp.concatenate([a0[:, :mid], a0[:, mid:] + a1], axis=1)

    for g in range(groups):
        for copy in in_copies[g]:
            copy.wait()
        pl.loop(0, heads, unroll=2)(functools.partial(conv_head, g))
        if g == groups - 2 and half > 1:
            gather[0].wait_recv()
            forward[1].start()
    for i in range(2, half):
        gather[i - 1].wait_recv()
        forward[i].start()
    for copy in forward:
        copy.wait_recv()

    def cart_head(g, j):
        cols = pl.ds(pl.multiple_of(g * width + j * HD, HD), HD)
        key = buf[:, g].reshape(cart, HD)
        value = buf[:, groups + g].reshape(cart, HD)
        q, og = q_s[:, cols], og_s[:, cols]
        h = g * heads + j
        x = dot_nt(key, q) * factor
        d = dot_nt(value, og)
        top_conv = stats[h, 0:1, :]
        top = jnp.maximum(jnp.max(x, axis=0, keepdims=True), top_conv)
        shrink = jnp.exp2(top_conv - top)
        e = jnp.exp2(x - top)
        total = stats[h, 1:2, :] * shrink + jnp.sum(e, axis=0, keepdims=True)
        weighted = stats[h, 2:3, :] * shrink + jnp.sum(e * d, axis=0, keepdims=True)
        inverse = 1.0 / total
        delta = weighted * inverse
        probs = e * inverse
        dscore = probs * (d - delta)
        part[g, :, :, 0] += dot(dscore.astype(jnp.bfloat16), q).reshape(half, 2, rows, HD)
        part[g, :, :, 1] += dot(probs.astype(jnp.bfloat16), og).reshape(half, 2, rows, HD)

    part[...] = jnp.zeros_like(part)
    peers = [lax.rem(me + 2 * i, n) for i in range(half)]
    pair_copies, place_copies, all_copies = [], [], []

    def start_pair(g):
        copy = remote(
            part.at[g, :, 1 - core], r1.at[g], s1_send.at[g], s1_recv.at[g], (dp, sibling)
        )
        copy.start()
        pair_copies.append(copy)

    def start_place(g):
        pair_copies[g].wait_recv()
        copies = []
        for i in range(1, half):
            to = lax.rem(place + i, half)
            s2[g, i] = (part[g, to, core] + r1[g, to]).astype(jnp.bfloat16)
            copy = remote(
                s2.at[g, i], r2.at[g, i], s2_send.at[g, i], s2_recv.at[g, i], (dp, peers[i])
            )
            copy.start()
            copies.append(copy)
        place_copies.append(copies)

    def start_all(g):
        total = part[g, place, core] + r1[g, place]
        for i in range(1, half):
            place_copies[g][i - 1].wait_recv()
            total = total + r2[g, i].astype(jnp.float32)
        r3[g, dp] = total.astype(jnp.bfloat16)
        copies = []
        for i in range(1, nd):
            copy = remote(
                r3.at[g, dp], r3.at[g, dp], s3_send.at[g, i], s3_recv.at[g, i],
                (lax.rem(dp + i, nd), me),
            )
            copy.start()
            copies.append(copy)
        all_copies.append(copies)

    def finish(g):
        for copy in all_copies[g]:
            copy.wait_recv()
        total = r3[g, 0].astype(jnp.float32)
        for i in range(1, nd):
            total = total + r3[g, i].astype(jnp.float32)
        dk_ref[:, g * HD : (g + 1) * HD] = total[0] * scale
        dv_ref[:, g * HD : (g + 1) * HD] = total[1]

    for g in range(groups):
        pl.loop(0, heads, unroll=2)(functools.partial(cart_head, g))
        start_pair(g)
        if g >= 1:
            start_place(g - 1)
        if g >= 2:
            start_all(g - 2)
    start_place(groups - 1)
    if groups > 1:
        start_all(groups - 2)
    for g in range(groups - 1):
        finish(g)
    start_all(groups - 1)
    finish(groups - 1)

    for copy in gather + forward + pair_copies:
        copy.wait_send()
    for copies in place_copies + all_copies:
        for copy in copies:
            copy.wait_send()


def solution(mesh):
    n, nd = mesh.shape["ctx"], mesh.shape["dp"]

    def per_device(queries, conv_keys, conv_values, out_grad, segment_ids, cart_keys, cart_values):
        tokens = queries.shape[0]
        rows = cart_keys.shape[0]
        groups = cart_keys.shape[1] // HD
        heads = queries.shape[1] // (groups * HD)
        half = n // 2
        bf16, f32 = jnp.bfloat16, jnp.float32
        dma = pltpu.SemaphoreType.DMA
        scratch = [
            pltpu.VMEM(queries.shape, bf16),
            pltpu.VMEM(out_grad.shape, bf16),
            pltpu.VMEM(conv_keys.shape, bf16),
            pltpu.VMEM(conv_values.shape, bf16),
            pltpu.VMEM(segment_ids.shape, jnp.int32),
            pltpu.VMEM((tokens, tokens), f32),
            pltpu.VMEM((groups * heads, 8, tokens), f32),
            pltpu.VMEM((n, 2 * groups, rows, HD), bf16),
            pltpu.VMEM((groups, half, 2, 2, rows, HD), f32),
            pltpu.VMEM((groups, half, 2, rows, HD), f32),
            pltpu.VMEM((groups, half, 2, rows, HD), bf16),
            pltpu.VMEM((groups, half, 2, rows, HD), bf16),
            pltpu.VMEM((groups, nd, 2, rows, HD), bf16),
            dma((2, groups)),
            dma((3,)),
            dma((2 * groups,)),
            dma((half,)),
            dma((half,)),
            dma((half,)),
            dma((half,)),
            dma((groups,)),
            dma((groups,)),
            dma((groups, half)),
            dma((groups, half)),
            dma((groups, nd)),
            dma((groups, nd)),
        ]
        return pl.pallas_call(
            functools.partial(kernel, n, nd, groups, heads),
            out_shape=[jax.ShapeDtypeStruct(cart_keys.shape, f32)] * 2,
            in_specs=[pl.BlockSpec(memory_space=pl.ANY)] * 7,
            out_specs=[pl.BlockSpec(memory_space=pltpu.VMEM)] * 2,
            scratch_shapes=scratch,
            compiler_params=pltpu.CompilerParams(
                collective_id=0, has_side_effects=True, vmem_limit_bytes=48 * 1024 * 1024
            ),
        )(queries, conv_keys, conv_values, out_grad, segment_ids, cart_keys, cart_values)

    in_specs = (P(("dp", "ctx"), None),) * 5 + (P("ctx", None),) * 2
    out_specs = (P("ctx", None), P("ctx", None))
    return jax.shard_map(
        per_device, mesh=mesh, in_specs=in_specs, out_specs=out_specs, check_vma=False
    )
```

time: 199 us -> 48.7 us (0.24)
  waiting for transfers between devices: 76.8 us -> 0 us
  matrix products: 47.3 us -> 0 us
  Pallas kernels: 0 us -> 39.2 us
  blocking collectives: 30.2 us -> 0 us
  between operations: 14.2 us -> 0.66 us
  local copies, waits for them, and re-layouts: 20 us -> 8.53 us
  other arithmetic: 8.29 us -> 0 us
    dot_general x28 -> x0, matrix products: 47.3 us -> none  [the longest x4 9.64 us: group_grads(): jnp.einsum('tgj,tgd->jd', dscore_b, query_group, preferred_element_type=j...]
    psum x1 -> x0, waiting for transfers between devices: 43.2 us -> none  [per_device(): summed = lax.psum(partial_sum, 'dp')]
    pallas_call x0 -> x1, Pallas kernels: none -> 39.2 us  [per_device(): pl.pallas_call(functools.partial(kernel, n, nd, groups, heads), out_shape...]
    reduce_scatter x1 -> x0, waiting for transfers between devices: 33.5 us -> none  [per_device(): lax.psum_scatter(jnp.concatenate([key_part, value_part], axis=1), 'ctx',...]
    all_gather x2 -> x0, blocking collectives: 30.2 us -> none  [the longest x1 16 us: per_device(): lax.all_gather(cart_values, 'ctx', axis=0, tiled=True)]
    reduce_sum x5 -> x0, other arithmetic: 6.73 us -> none  [the longest x1 3.55 us: per_device(): deltas = jnp.sum(grad_heads.astype(jnp.float32) * mixed, axis=-1)]
    dynamic_update_slice x8 -> x0, local copies, waits for them, and re-layouts: 5.79 us -> none  [per_device(): lax.map(lambda items: group_stats(items, allowed, scale), (query_heads, s...]
    while x2 -> x0, local copies, waits for them, and re-layouts: 2.57 us -> none  [per_device(): lax.map(lambda items: group_grads(items, scale), (query_heads, grad_heads...]
  transfers between devices with their start and end apart: 2 -> 0, of which waited for: 2 -> 0; matrix products, arithmetic and copies ran while one was open for 0% -> 0% of each run, Pallas kernels for 0% -> 0%
where the time goes in v1:
time: 48.7 us; the launch traced here: 48.3 us
  Pallas kernels  39.2 us (80%)
  local copies, waits for them, and re-layouts  8.53 us (18%)
  between operations  0.66 us (1%)
    pallas_call x1, Pallas kernels, per_device(): pl.pallas_call(functools.partial(kernel, n, nd, groups, heads), out_shape...  39.2 us
    unnamed x16, local copies, waits for them, and re-layouts  8.53 us

profile of v1, /device:TPU:0, one launch (start us, length us, event | category | flops | bytes accessed | tf_op | source)
XLA Modules:
  0.0 48.3 jit_solution(12320085883589704000)
XLA Ops:
  0.6 0.0 copy-start
  0.6 1.6 %copy-done = bf16[256,4096]{1,0:T(8,128)(2,1)S(1)} copy-done((bf16[256,4096]{1,0:T(8,128)(2,1)S(1)}, bf16[256,4096]{1,0:T(8,128)(2,1)}, u32[]{:S(2)}) %copy-start) | copy-done | bytes 2097176
  2.2 0.0 copy-start.1
  2.2 1.6 %copy-done.1 = bf16[256,4096]{1,0:T(8,128)(2,1)S(1)} copy-done((bf16[256,4096]{1,0:T(8,128)(2,1)S(1)}, bf16[256,4096]{1,0:T(8,128)(2,1)}, u32[]{:S(2)}) %copy-start.1) | copy-done | bytes 2097176
  3.8 0.0 copy-start.2
  3.8 0.9 %copy-done.2 = bf16[256,512]{1,0:T(8,128)(2,1)S(1)} copy-done((bf16[256,512]{1,0:T(8,128)(2,1)S(1)}, bf16[256,512]{1,0:T(8,128)(2,1)}, u32[]{:S(2)}) %copy-start.2) | copy-done | bytes 262168
  4.8 0.0 copy-start.3
  4.8 0.9 %copy-done.3 = bf16[256,512]{1,0:T(8,128)(2,1)S(1)} copy-done((bf16[256,512]{1,0:T(8,128)(2,1)S(1)}, bf16[256,512]{1,0:T(8,128)(2,1)}, u32[]{:S(2)}) %copy-start.3) | copy-done | bytes 262168
  5.7 0.0 copy-start.4
  5.7 0.8 %copy-done.4 = bf16[32,512]{1,0:T(8,128)(2,1)S(1)} copy-done((bf16[32,512]{1,0:T(8,128)(2,1)S(1)}, bf16[32,512]{1,0:T(8,128)(2,1)}, u32[]{:S(2)}) %copy-start.4) | copy-done | bytes 32792
  6.5 0.0 copy-start.5
  6.5 0.8 %copy-done.5 = bf16[32,512]{1,0:T(8,128)(2,1)S(1)} copy-done((bf16[32,512]{1,0:T(8,128)(2,1)S(1)}, bf16[32,512]{1,0:T(8,128)(2,1)}, u32[]{:S(2)}) %copy-start.5) | copy-done | bytes 32792
  7.2 0.0 copy-start.6
  7.2 0.7 %copy-done.6 = s32[1,256]{1,0:T(1,128)S(1)} copy-done((s32[1,256]{1,0:T(1,128)S(1)}, s32[1,256]{1,0:T(1,128)}, u32[]{:S(2)}) %copy-start.6) | copy-done | bytes 1048
  7.9 39.2 %shard_map.86 = (f32[32,512]{1,0:T(8,128)S(1)}, f32[32,512]{1,0:T(8,128)S(1)}) custom-call(bf16[256,4096]{1,0:T(8,128)(2,1)S(1)} %copy-done, bf16[256,512]{1,0:T(8,128)(2,1)S(1)} %copy-done.2, bf16[256,512]{1,0:T(8,128)(2,1)S(1)} %copy-done.3, bf16[256,4096]{1,0:T(8,128)(2,1)S(1)} %copy-done.1, s32[1,256]{1,0:T(1,128)S(1)} %copy-done.6, ...), custom_call_target="tpu_custom_call" | custom-call | tf_op jit(solution)/shard_map/pallas_call | solution.py:287
  47.1 0.6 %copy.11 = f32[32,512]{1,0:T(8,128)} copy(f32[32,512]{1,0:T(8,128)S(1)} %get-tuple-element.4) | data formatting | bytes 131072
  47.7 0.6 %copy.12 = f32[32,512]{1,0:T(8,128)} copy(f32[32,512]{1,0:T(8,128)S(1)} %get-tuple-element.5) | data formatting | bytes 131072
Async XLA Ops:
  0.6 1.6 %copy-start = (bf16[256,4096]{1,0:T(8,128)(2,1)S(1)}, bf16[256,4096]{1,0:T(8,128)(2,1)}, u32[]{:S(2)}) copy-start(bf16[256,4096]{1,0:T(8,128)(2,1)} %q_hbm.1) | copy-start | bytes 6291460
  2.2 1.6 %copy-start.1 = (bf16[256,4096]{1,0:T(8,128)(2,1)S(1)}, bf16[256,4096]{1,0:T(8,128)(2,1)}, u32[]{:S(2)}) copy-start(bf16[256,4096]{1,0:T(8,128)(2,1)} %og_hbm.1) | copy-start | bytes 6291460
  3.8 0.9 %copy-start.2 = (bf16[256,512]{1,0:T(8,128)(2,1)S(1)}, bf16[256,512]{1,0:T(8,128)(2,1)}, u32[]{:S(2)}) copy-start(bf16[256,512]{1,0:T(8,128)(2,1)} %ck_hbm.1) | copy-start | bytes 786436
  4.8 0.9 %copy-start.3 = (bf16[256,512]{1,0:T(8,128)(2,1)S(1)}, bf16[256,512]{1,0:T(8,128)(2,1)}, u32[]{:S(2)}) copy-start(bf16[256,512]{1,0:T(8,128)(2,1)} %cv_hbm.1) | copy-start | bytes 786436
  5.7 0.8 %copy-start.4 = (bf16[32,512]{1,0:T(8,128)(2,1)S(1)}, bf16[32,512]{1,0:T(8,128)(2,1)}, u32[]{:S(2)}) copy-start(bf16[32,512]{1,0:T(8,128)(2,1)} %kk_hbm.1) | copy-start | bytes 98308
  6.5 0.8 %copy-start.5 = (bf16[32,512]{1,0:T(8,128)(2,1)S(1)}, bf16[32,512]{1,0:T(8,128)(2,1)}, u32[]{:S(2)}) copy-start(bf16[32,512]{1,0:T(8,128)(2,1)} %kv_hbm.1) | copy-start | bytes 98308
  7.2 0.7 %copy-start.6 = (s32[1,256]{1,0:T(1,128)S(1)}, s32[1,256]{1,0:T(1,128)}, u32[]{:S(2)}) copy-start(s32[1,256]{1,0:T(1,128)} %seg_hbm.1) | copy-start | bytes 3076

commit v2 on v1

--- a/solution.py
+++ b/solution.py
@@ -26,6 +26,7 @@
     q_hbm, ck_hbm, cv_hbm, og_hbm, seg_hbm, kk_hbm, kv_hbm,
     dk_ref, dv_ref,
     q_s, og_s, ck_s, cv_s, seg_s, bias, stats, buf, part, r1, s2, r2, r3,
+    score_a, score_b, dprob_a, dprob_b, tops_a, tops_b, probs_a, probs_b, dscore_a, dscore_b,
     in_sem, conv_sem, cart_sem,
     g_send, g_recv, f_send, f_recv, s1_send, s1_recv, s2_send, s2_recv, s3_send, s3_recv,
 ):
@@ -41,6 +42,9 @@
     scale = 1.0 / math.sqrt(HD)
     factor = scale * math.log2(math.e)
 
+    score, dprob, tops = (score_a, score_b), (dprob_a, dprob_b), (tops_a, tops_b)
+    probs, dscore = (probs_a, probs_b), (dscore_a, dscore_b)
+
     barrier = pltpu.get_barrier_semaphore()
     pl.semaphore_signal(barrier, inc=1, device_id=(dp, sibling), device_id_type=MESH)
     for i in range(1, half):
@@ -72,16 +76,16 @@
     ]
     for copy in conv_copies:
         copy.start()
-    in_copies = []
+
+    def in_copies(g):
+        cols = pl.ds(pl.multiple_of(g * width, width), width)
+        return [
+            pltpu.make_async_copy(q_hbm.at[:, cols], q_s.at[:, cols], in_sem.at[0, g]),
+            pltpu.make_async_copy(og_hbm.at[:, cols], og_s.at[:, cols], in_sem.at[1, g]),
+        ]
+
     for g in range(groups):
-        cols = pl.ds(g * width, width)
-        in_copies.append(
-            (
-                pltpu.make_async_copy(q_hbm.at[:, cols], q_s.at[:, cols], in_sem.at[0, g]),
-                pltpu.make_async_copy(og_hbm.at[:, cols], og_s.at[:, cols], in_sem.at[1, g]),
-            )
-        )
-        for copy in in_copies[-1]:
+        for copy in in_copies(g):
             copy.start()
     for copy in cart_copies:
         copy.wait()
@@ -117,119 +121,174 @@
     bias[...] = jnp.where(allowed, 0.0, -1e30)
     mid = tokens // 2
 
-    def conv_head(g, j):
-        cols = pl.ds(pl.multiple_of(g * width + j * HD, HD), HD)
-        key = ck_s[:, g * HD : (g + 1) * HD]
-        value = cv_s[:, g * HD : (g + 1) * HD]
+    strip = 32
+
+    def fold(x, reduce):
+        return reduce(x.reshape(x.shape[0] // 8, 8, x.shape[1]), axis=0)
+
+    def head_cols(g, j):
+        return pl.ds(pl.multiple_of(g * width + j * HD, HD), HD)
+
+    def conv_products(g, j, slot):
+        cols, own = head_cols(g, j), pl.ds(pl.multiple_of(g * HD, HD), HD)
         q, og = q_s[:, cols], og_s[:, cols]
-        x0 = dot_nt(key[:mid], q) * factor + bias[:mid, :]
-        x1 = dot_nt(key[mid:], q[mid:]) * factor + bias[mid:, mid:]
-        d0 = dot_nt(value[:mid], og)
-        d1 = dot_nt(value[mid:], og[mid:])
-        top0 = jnp.max(x0, axis=0, keepdims=True)
-        top1 = jnp.max(x1, axis=0, keepdims=True)
-        top = jnp.concatenate([top0[:, :mid], jnp.maximum(top0[:, mid:], top1)], axis=1)
-        e0 = jnp.exp2(x0 - top)
-        e1 = jnp.exp2(x1 - top[:, mid:])
-        l0 = jnp.sum(e0, axis=0, keepdims=True)
-        l1 = jnp.sum(e1, axis=0, keepdims=True)
-        a0 = jnp.sum(e0 * d0, axis=0, keepdims=True)
-        a1 = jnp.sum(e1 * d1, axis=0, keepdims=True)
+        s0 = dot_nt(ck_s[:mid, own], q) + bias[:mid, :]
+        s1 = dot_nt(ck_s[mid:, own], q[mid:]) + bias[mid:, mid:]
+        score[slot][:mid, :] = s0
+        score[slot][mid:tokens, mid:] = s1
+        dprob[slot][:mid, :] = dot_nt(cv_s[:mid, own], og)
+        dprob[slot][mid:tokens, mid:] = dot_nt(cv_s[mid:, own], og[mid:])
+        top0 = jnp.max(fold(s0, jnp.max), axis=0, keepdims=True)
+        top1 = jnp.max(fold(s1, jnp.max), axis=0, keepdims=True)
+        tops[slot][0:1, :] = jnp.concatenate(
+            [top0[:, :mid], jnp.maximum(top0[:, mid:], top1)], axis=1
+        ) * factor
+
+    def conv_sums(g, j, slot):
+        top = tops[slot][0:1, :]
+        total = weighted = None
+        for low in range(0, mid, strip):
+            e = jnp.exp2(score[slot][low : low + strip, :] * factor - top)
+            w = e * dprob[slot][low : low + strip, :]
+            e, w = fold(e, jnp.sum), fold(w, jnp.sum)
+            total, weighted = (e, w) if total is None else (total + e, weighted + w)
+        late_total = late_weighted = None
+        for low in range(mid, tokens, strip):
+            e = jnp.exp2(score[slot][low : low + strip, mid:] * factor - top[:, mid:])
+            w = e * dprob[slot][low : low + strip, mid:]
+            e, w = fold(e, jnp.sum), fold(w, jnp.sum)
+            late_total, late_weighted = (
+                (e, w) if late_total is None else (late_total + e, late_weighted + w)
+            )
+
+        def whole(early, late):
+            both = jnp.concatenate([early[:, :mid], early[:, mid:] + late], axis=1)
+            return jnp.sum(both, axis=0, keepdims=True)
+
         h = g * heads + j
         stats[h, 0:1, :] = top
-        stats[h, 1:2, :] = jnp.concatenate([l0[:, :mid], l0[:, mid:] + l1], axis=1)
-        stats[h, 2:3, :] = jnp.concatenate([a0[:, :mid], a0[:, mid:] + a1], axis=1)
-
-    for g in range(groups):
-        for copy in in_copies[g]:
+        stats[h, 1:2, :] = whole(total, late_total)
+        stats[h, 2:3, :] = whole(weighted, late_weighted)
+
+    def conv_group(g):
+        for copy in in_copies(g):
             copy.wait()
-        pl.loop(0, heads, unroll=2)(functools.partial(conv_head, g))
-        if g == groups - 2 and half > 1:
-            gather[0].wait_recv()
-            forward[1].start()
+        conv_products(g, 0, 0)
+        for j in range(heads):
+            if j + 1 < heads:
+                conv_products(g, j + 1, (j + 1) % 2)
+            conv_sums(g, j, j % 2)
+
+        if half > 1:
+            @pl.when(g == groups - 2)
+            def _():
+                gather[0].wait_recv()
+                forward[1].start()
+
+    pl.loop(0, groups)(conv_group)
     for i in range(2, half):
         gather[i - 1].wait_recv()
         forward[i].start()
     for copy in forward:
         copy.wait_recv()
 
-    def cart_head(g, j):
-        cols = pl.ds(pl.multiple_of(g * width + j * HD, HD), HD)
-        key = buf[:, g].reshape(cart, HD)
-        value = buf[:, groups + g].reshape(cart, HD)
-        q, og = q_s[:, cols], og_s[:, cols]
+    def cart_products(g, j, slot):
+        cols = head_cols(g, j)
+        s = dot_nt(buf[:, g].reshape(cart, HD), q_s[:, cols])
+        score[slot][:cart, :] = s
+        tops[slot][0:1, :] = jnp.max(fold(s, jnp.max), axis=0, keepdims=True) * factor
+        dprob[slot][:cart, :] = dot_nt(buf[:, groups + g].reshape(cart, HD), og_s[:, cols])
+
+    def cart_probs(g, j, slot):
         h = g * heads + j
-        x = dot_nt(key, q) * factor
-        d = dot_nt(value, og)
         top_conv = stats[h, 0:1, :]
-        top = jnp.maximum(jnp.max(x, axis=0, keepdims=True), top_conv)
+        top = jnp.maximum(tops[slot][0:1, :], top_conv)
+        total = weighted = None
+        for low in range(0, cart, strip):
+            e = jnp.exp2(score[slot][low : low + strip, :] * factor - top)
+            score[slot][low : low + strip, :] = e
+            w = e * dprob[slot][low : low + strip, :]
+            e, w = fold(e, jnp.sum), fold(w, jnp.sum)
+            total, weighted = (e, w) if total is None else (total + e, weighted + w)
         shrink = jnp.exp2(top_conv - top)
-        e = jnp.exp2(x - top)
-        total = stats[h, 1:2, :] * shrink + jnp.sum(e, axis=0, keepdims=True)
-        weighted = stats[h, 2:3, :] * shrink + jnp.sum(e * d, axis=0, keepdims=True)
+        total = stats[h, 1:2, :] * shrink + jnp.sum(total, axis=0, keepdims=True)
+        weighted = stats[h, 2:3, :] * shrink + jnp.sum(weighted, axis=0, keepdims=True)
         inverse = 1.0 / total
         delta = weighted * inverse
-        probs = e * inverse
-        dscore = probs * (d - delta)
-        part[g, :, :, 0] += dot(dscore.astype(jnp.bfloat16), q).reshape(half, 2, rows, HD)
-        part[g, :, :, 1] += dot(probs.astype(jnp.bfloat16), og).reshape(half, 2, rows, HD)
-
-    part[...] = jnp.zeros_like(part)
+        for low in range(0, cart, strip):
+            p = score[slot][low : low + strip, :] * inverse
+            probs[slot][low : low + strip, :] = p.astype(jnp.bfloat16)
+            ds = p * (dprob[slot][low : low + strip, :] - delta)
+            dscore[slot][low : low + strip, :] = ds.astype(jnp.bfloat16)
+
+    def cart_grads(g, j, slot):
+        cols = head_cols(g, j)
+        for kind, (left, right) in enumerate(((dscore, q_s), (probs, og_s))):
+            term = dot(left[slot][...], right[:, cols]).reshape(half, 2, rows, HD)
+            if j > 0:
+                term = part[g, :, :, kind] + term
+            part[g, :, :, kind] = term
+
     peers = [lax.rem(me + 2 * i, n) for i in range(half)]
-    pair_copies, place_copies, all_copies = [], [], []
-
-    def start_pair(g):
-        copy = remote(
+    def pair_copy(g):
+        return remote(
             part.at[g, :, 1 - core], r1.at[g], s1_send.at[g], s1_recv.at[g], (dp, sibling)
         )
-        copy.start()
-        pair_copies.append(copy)
+
+    def place_copy(g, i):
+        return remote(
+            s2.at[g, i], r2.at[g, i], s2_send.at[g, i], s2_recv.at[g, i], (dp, peers[i])
+        )
+
+    def all_copy(g, i):
+        return remote(
+            r3.at[g, dp], r3.at[g, dp], s3_send.at[g, i], s3_recv.at[g, i],
+            (lax.rem(dp + i, nd), me),
+        )
 
     def start_place(g):
-        pair_copies[g].wait_recv()
-        copies = []
+        pair_copy(g).wait_recv()
         for i in range(1, half):
             to = lax.rem(place + i, half)
             s2[g, i] = (part[g, to, core] + r1[g, to]).astype(jnp.bfloat16)
-            copy = remote(
-                s2.at[g, i], r2.at[g, i], s2_send.at[g, i], s2_recv.at[g, i], (dp, peers[i])
-            )
-            copy.start()
-            copies.append(copy)
-        place_copies.append(copies)
+            place_copy(g, i).start()
 
     def start_all(g):
         total = part[g, place, core] + r1[g, place]
         for i in range(1, half):
-            place_copies[g][i - 1].wait_recv()
+            place_copy(g, i).wait_recv()
             total = total + r2[g, i].astype(jnp.float32)
         r3[g, dp] = total.astype(jnp.bfloat16)
-        copies = []
         for i in range(1, nd):
-            copy = remote(
-                r3.at[g, dp], r3.at[g, dp], s3_send.at[g, i], s3_recv.at[g, i],
-                (lax.rem(dp + i, nd), me),
-            )
-            copy.start()
-            copies.append(copy)
-        all_copies.append(copies)
+            all_copy(g, i).start()
 
     def finish(g):
-        for copy in all_copies[g]:
-            copy.wait_recv()
+        for i in range(1, nd):
+            all_copy(g, i).wait_recv()
         total = r3[g, 0].astype(jnp.float32)
         for i in range(1, nd):
             total = total + r3[g, i].astype(jnp.float32)
         dk_ref[:, g * HD : (g + 1) * HD] = total[0] * scale
         dv_ref[:, g * HD : (g + 1) * HD] = total[1]
 
-    for g in range(groups):
-        pl.loop(0, heads, unroll=2)(functools.partial(cart_head, g))
-        start_pair(g)
-        if g >= 1:
+    def cart_group(g):
+        cart_products(g, 0, 0)
+        for j in range(heads):
+            if j + 1 < heads:
+                cart_products(g, j + 1, (j + 1) % 2)
+            cart_probs(g, j, j % 2)
+            cart_grads(g, j, j % 2)
+        pair_copy(g).start()
+
+        @pl.when(g >= 1)
+        def _():
             start_place(g - 1)
-        if g >= 2:
+
+        @pl.when(g >= 2)
+        def _():
             start_all(g - 2)
+
+    pl.loop(0, groups)(cart_group)
     start_place(groups - 1)
     if groups > 1:
         start_all(groups - 2)
@@ -238,11 +297,14 @@
     start_all(groups - 1)
     finish(groups - 1)
 
-    for copy in gather + forward + pair_copies:
+    for copy in gather + forward:
         copy.wait_send()
-    for copies in place_copies + all_copies:
-        for copy in copies:
-            copy.wait_send()
+    for g in range(groups):
+        pair_copy(g).wait_send()
+        for i in range(1, half):
+            place_copy(g, i).wait_send()
+        for i in range(1, nd):
+            all_copy(g, i).wait_send()
 
 
 def solution(mesh):
@@ -270,6 +332,9 @@
             pltpu.VMEM((groups, half, 2, rows, HD), bf16),
             pltpu.VMEM((groups, half, 2, rows, HD), bf16),
             pltpu.VMEM((groups, nd, 2, rows, HD), bf16),
+            *[pltpu.VMEM((max(n * rows, tokens), tokens), f32)] * 4,
+            *[pltpu.VMEM((8, tokens), f32)] * 2,
+            *[pltpu.VMEM((n * rows, tokens), bf16)] * 4,
             dma((2, groups)),
             dma((3,)),
             dma((2 * groups,)),
@@ -287,11 +352,11 @@
         return pl.pallas_call(
             functools.partial(kernel, n, nd, groups, heads),
             out_shape=[jax.ShapeDtypeStruct(cart_keys.shape, f32)] * 2,
-            in_specs=[pl.BlockSpec(memory_space=pl.ANY)] * 7,
+            in_specs=[pl.BlockSpec(memory_space=pltpu.HBM)] * 7,
             out_specs=[pl.BlockSpec(memory_space=pltpu.VMEM)] * 2,
             scratch_shapes=scratch,
             compiler_params=pltpu.CompilerParams(
-                collective_id=0, has_side_effects=True, vmem_limit_bytes=48 * 1024 * 1024
+                collective_id=0, has_side_effects=True, vmem_limit_bytes=64 * 1024 * 1024
             ),
         )(queries, conv_keys, conv_values, out_grad, segment_ids, cart_keys, cart_values)
 

time: 48.7 us -> 38.3 us (0.79)
  local copies, waits for them, and re-layouts: 8.53 us -> 2.95 us
  Pallas kernels: 39.2 us -> 34.5 us
    unnamed x16 -> x2, local copies, waits for them, and re-layouts: 8.53 us -> 2.95 us
    pallas_call x1, Pallas kernels: 39.2 us -> 34.5 us  [per_device(): pl.pallas_call(functools.partial(kernel, n, nd, groups, heads), out_shape...]
where the time goes in v2:
time: 38.3 us; the launch traced here: 38.1 us
  Pallas kernels  34.5 us (90%)
  local copies, waits for them, and re-layouts  2.95 us (8%)
  between operations  0.64 us (2%)
    pallas_call x1, Pallas kernels, per_device(): pl.pallas_call(functools.partial(kernel, n, nd, groups, heads), out_shape...  34.5 us
    unnamed x2, local copies, waits for them, and re-layouts  2.95 us

profile of v2, /device:TPU:0, one launch (start us, length us, event | category | flops | bytes accessed | tf_op | source)
XLA Modules:
  0.0 38.1 jit_solution(16409179235084450405)
XLA Ops:
  0.6 34.5 %shard_map.86 = (f32[32,512]{1,0:T(8,128)}, f32[32,512]{1,0:T(8,128)}) custom-call(bf16[256,4096]{1,0:T(8,128)(2,1)} %q_hbm.1, bf16[256,512]{1,0:T(8,128)(2,1)} %ck_hbm.1, bf16[256,512]{1,0:T(8,128)(2,1)} %cv_hbm.1, bf16[256,4096]{1,0:T(8,128)(2,1)} %og_hbm.1, s32[1,256]{1,0:T(1,128)} %seg_hbm.1, bf16[32,512]{1,0:T(8,128)(2,1)} %kk_hbm.1, bf16[32,512]{1,0:T(8,128)(2,1)} %kv_hbm.1), custom_call_target="tpu_custom_call" | custom-call | tf_op jit(solution)/shard_map/pallas_call | solution.py:352
  35.1 1.5 %copy.11 = f32[32,512]{1,0:T(8,128)} copy(f32[32,512]{1,0:T(8,128)} %get-tuple-element.4) | data formatting | bytes 131072
  36.6 1.5 %copy.12 = f32[32,512]{1,0:T(8,128)} copy(f32[32,512]{1,0:T(8,128)} %get-tuple-element.5) | data formatting | bytes 131072

commit v3 on v2

--- a/solution.py
+++ b/solution.py
@@ -24,7 +24,7 @@
 def kernel(
     n, nd, groups, heads,
     q_hbm, ck_hbm, cv_hbm, og_hbm, seg_hbm, kk_hbm, kv_hbm,
-    dk_ref, dv_ref,
+    out_ref,
     q_s, og_s, ck_s, cv_s, seg_s, bias, stats, buf, part, r1, s2, r2, r3,
     score_a, score_b, dprob_a, dprob_b, tops_a, tops_b, probs_a, probs_b, dscore_a, dscore_b,
     in_sem, conv_sem, cart_sem,
@@ -36,11 +36,10 @@
     place = me // 2
     sibling = me + 1 - 2 * core
     tokens = q_s.shape[0]
-    rows = buf.shape[2]
+    rows = buf.shape[3]
     cart = n * rows
     width = heads * HD
-    scale = 1.0 / math.sqrt(HD)
-    factor = scale * math.log2(math.e)
+    factor = math.log2(math.e) / math.sqrt(HD)
 
     score, dprob, tops = (score_a, score_b), (dprob_a, dprob_b), (tops_a, tops_b)
     probs, dscore = (probs_a, probs_b), (dscore_a, dscore_b)
@@ -59,14 +58,12 @@
     cart_copies = []
     for g in range(groups):
         cols = pl.ds(g * HD, HD)
-        cart_copies.append(
-            pltpu.make_async_copy(kk_hbm.at[:, cols], buf.at[me, g], cart_sem.at[g])
-        )
-        cart_copies.append(
-            pltpu.make_async_copy(
-                kv_hbm.at[:, cols], buf.at[me, groups + g], cart_sem.at[groups + g]
+        for kind, ref in enumerate((kk_hbm, kv_hbm)):
+            cart_copies.append(
+                pltpu.make_async_copy(
+                    ref.at[:, cols], buf.at[g, me, kind], cart_sem.at[kind, g]
+                )
             )
-        )
     for copy in cart_copies:
         copy.start()
     conv_copies = [
@@ -97,20 +94,29 @@
             device_id=target, device_id_type=MESH,
         )
 
-    gather = [
-        remote(
-            buf.at[me], buf.at[me], g_send.at[i], g_recv.at[i], (dp, lax.rem(me + 2 * i, n))
-        )
-        for i in range(1, half)
-    ]
-    arrivals = [lax.rem(me + n - 2 * i, n) for i in range(half)]
-    forward = [
-        remote(buf.at[a], buf.at[a], f_send.at[i], f_recv.at[i], (dp, sibling))
-        for i, a in enumerate(arrivals)
-    ]
-    for copy in gather:
-        copy.start()
-    forward[0].start()
+    def gather(g, i):
+        return remote(
+            buf.at[g, me], buf.at[g, me], g_send.at[g, i], g_recv.at[g, i],
+            (dp, lax.rem(me + 2 * i, n)),
+        )
+
+    def forward(g, i):
+        chunk = buf.at[g, lax.rem(me + n - 2 * i, n)]
+        return remote(chunk, chunk, f_send.at[g, i], f_recv.at[g, i], (dp, sibling))
+
+    def pass_on(g):
+        for i in range(1, half):
+            gather(g, i).wait_recv()
+            forward(g, i).start()
+
+    def gathered(g):
+        for i in range(half):
+            forward(g, i).wait_recv()
+
+    for g in range(groups):
+        for i in range(1, half):
+            gather(g, i).start()
+        forward(g, 0).start()
 
     for copy in conv_copies:
         copy.wait()
@@ -170,34 +176,40 @@
         stats[h, 1:2, :] = whole(total, late_total)
         stats[h, 2:3, :] = whole(weighted, late_weighted)
 
-    def conv_group(g):
-        for copy in in_copies(g):
-            copy.wait()
-        conv_products(g, 0, 0)
-        for j in range(heads):
-            if j + 1 < heads:
-                conv_products(g, j + 1, (j + 1) % 2)
-            conv_sums(g, j, j % 2)
-
-        if half > 1:
-            @pl.when(g == groups - 2)
-            def _():
-                gather[0].wait_recv()
-                forward[1].start()
-
-    pl.loop(0, groups)(conv_group)
-    for i in range(2, half):
-        gather[i - 1].wait_recv()
-        forward[i].start()
-    for copy in forward:
-        copy.wait_recv()
+    per = heads // 2
+
+    def next_of(step, j):
+        head = jnp.minimum(step * per + j + 1, groups * heads - 1)
+        return head // heads, lax.rem(head, heads)
+
+    def conv_step(step):
+        g, first = step // 2, lax.rem(step, 2) * per
+
+        @pl.when((first > 0) & (g + 1 < groups))
+        def _():
+            for copy in in_copies(g + 1):
+                copy.wait()
+
+        for j in range(per):
+            conv_products(*next_of(step, j), (j + 1) % 2)
+            conv_sums(g, first + j, j % 2)
+
+        @pl.when((first > 0) & (g >= 1))
+        def _():
+            pass_on(g - 1)
+
+    for copy in in_copies(0):
+        copy.wait()
+    conv_products(0, 0, 0)
+    pl.loop(0, 2 * groups)(conv_step)
+    pass_on(groups - 1)
 
     def cart_products(g, j, slot):
         cols = head_cols(g, j)
-        s = dot_nt(buf[:, g].reshape(cart, HD), q_s[:, cols])
+        s = dot_nt(buf[g, :, 0].reshape(cart, HD), q_s[:, cols])
         score[slot][:cart, :] = s
         tops[slot][0:1, :] = jnp.max(fold(s, jnp.max), axis=0, keepdims=True) * factor
-        dprob[slot][:cart, :] = dot_nt(buf[:, groups + g].reshape(cart, HD), og_s[:, cols])
+        dprob[slot][:cart, :] = dot_nt(buf[g, :, 1].reshape(cart, HD), og_s[:, cols])
 
     def cart_probs(g, j, slot):
         h = g * heads + j
@@ -225,10 +237,9 @@
         cols = head_cols(g, j)
         for kind, (left, right) in enumerate(((dscore, q_s), (probs, og_s))):
             term = dot(left[slot][...], right[:, cols]).reshape(half, 2, rows, HD)
-            if j > 0:
-                term = part[g, :, :, kind] + term
-            part[g, :, :, kind] = term
-
+            part[g, :, :, kind] += term
+
+    part[...] = jnp.zeros_like(part)
     peers = [lax.rem(me + 2 * i, n) for i in range(half)]
     def pair_copy(g):
         return remote(
@@ -268,27 +279,35 @@
         total = r3[g, 0].astype(jnp.float32)
         for i in range(1, nd):
             total = total + r3[g, i].astype(jnp.float32)
-        dk_ref[:, g * HD : (g + 1) * HD] = total[0] * scale
-        dv_ref[:, g * HD : (g + 1) * HD] = total[1]
-
-    def cart_group(g):
-        cart_products(g, 0, 0)
-        for j in range(heads):
-            if j + 1 < heads:
-                cart_products(g, j + 1, (j + 1) % 2)
-            cart_probs(g, j, j % 2)
-            cart_grads(g, j, j % 2)
-        pair_copy(g).start()
-
-        @pl.when(g >= 1)
+        out_ref[:, :, g * HD : (g + 1) * HD] = total
+
+    def cart_step(step):
+        g, first = step // 2, lax.rem(step, 2) * per
+
+        @pl.when((first > 0) & (g + 1 < groups))
+        def _():
+            gathered(g + 1)
+
+        for j in range(per):
+            cart_products(*next_of(step, j), (j + 1) % 2)
+            cart_probs(g, first + j, j % 2)
+            cart_grads(g, first + j, j % 2)
+
+        @pl.when(first > 0)
+        def _():
+            pair_copy(g).start()
+
+        @pl.when((first == 0) & (g >= 1))
         def _():
             start_place(g - 1)
 
-        @pl.when(g >= 2)
+        @pl.when((first == 0) & (g >= 2))
         def _():
             start_all(g - 2)
 
-    pl.loop(0, groups)(cart_group)
+    gathered(0)
+    cart_products(0, 0, 0)
+    pl.loop(0, 2 * groups)(cart_step)
     start_place(groups - 1)
     if groups > 1:
         start_all(groups - 2)
@@ -297,9 +316,11 @@
     start_all(groups - 1)
     finish(groups - 1)
 
-    for copy in gather + forward:
-        copy.wait_send()
     for g in range(groups):
+        for i in range(1, half):
+            gather(g, i).wait_send()
+        for i in range(half):
+            forward(g, i).wait_send()
         pair_copy(g).wait_send()
         for i in range(1, half):
             place_copy(g, i).wait_send()
@@ -326,7 +347,7 @@
             pltpu.VMEM(segment_ids.shape, jnp.int32),
             pltpu.VMEM((tokens, tokens), f32),
             pltpu.VMEM((groups * heads, 8, tokens), f32),
-            pltpu.VMEM((n, 2 * groups, rows, HD), bf16),
+            pltpu.VMEM((groups, n, 2, rows, HD), bf16),
             pltpu.VMEM((groups, half, 2, 2, rows, HD), f32),
             pltpu.VMEM((groups, half, 2, rows, HD), f32),
             pltpu.VMEM((groups, half, 2, rows, HD), bf16),
@@ -337,11 +358,8 @@
             *[pltpu.VMEM((n * rows, tokens), bf16)] * 4,
             dma((2, groups)),
             dma((3,)),
-            dma((2 * groups,)),
-            dma((half,)),
-            dma((half,)),
-            dma((half,)),
-            dma((half,)),
+            dma((2, groups)),
+            *[dma((groups, half))] * 4,
             dma((groups,)),
             dma((groups,)),
             dma((groups, half)),
@@ -349,16 +367,17 @@
             dma((groups, nd)),
             dma((groups, nd)),
         ]
-        return pl.pallas_call(
+        out = pl.pallas_call(
             functools.partial(kernel, n, nd, groups, heads),
-            out_shape=[jax.ShapeDtypeStruct(cart_keys.shape, f32)] * 2,
+            out_shape=jax.ShapeDtypeStruct((2, *cart_keys.shape), f32),
             in_specs=[pl.BlockSpec(memory_space=pltpu.HBM)] * 7,
-            out_specs=[pl.BlockSpec(memory_space=pltpu.VMEM)] * 2,
+            out_specs=pl.BlockSpec(memory_space=pltpu.VMEM),
             scratch_shapes=scratch,
             compiler_params=pltpu.CompilerParams(
                 collective_id=0, has_side_effects=True, vmem_limit_bytes=64 * 1024 * 1024
             ),
         )(queries, conv_keys, conv_values, out_grad, segment_ids, cart_keys, cart_values)
+        return out[0] * (1.0 / math.sqrt(HD)), out[1]
 
     in_specs = (P(("dp", "ctx"), None),) * 5 + (P("ctx", None),) * 2
     out_specs = (P("ctx", None), P("ctx", None))

time: 38.3 us -> 37 us (0.966)
  local copies, waits for them, and re-layouts: 2.95 us -> 0 us
  other arithmetic: 0 us -> 1.53 us
    unnamed x2 -> x0, local copies, waits for them, and re-layouts: 2.95 us -> none
    squeeze x0 -> x1, other arithmetic: none -> 1.53 us  [per_device(): return (out[0] * (1.0 / math.sqrt(HD)), out[1])]
where the time goes in v3:
time: 37 us; the launch traced here: 36.8 us
  Pallas kernels  34.7 us (94%)
  other arithmetic  1.53 us (4%)
  between operations  0.64 us (2%)
    pallas_call x1, Pallas kernels, per_device(): pl.pallas_call(functools.partial(kernel, n, nd, groups, heads), out_shape...  34.7 us
    squeeze x1, other arithmetic, per_device(): return (out[0] * (1.0 / math.sqrt(HD)), out[1])  1.53 us

profile of v3, /device:TPU:0, one launch (start us, length us, event | category | flops | bytes accessed | tf_op | source)
XLA Modules:
  0.0 36.8 jit_solution(3287747671299851622)
XLA Ops:
  0.6 34.7 %shard_map.86 = f32[2,32,512]{2,1,0:T(8,128)} custom-call(bf16[256,4096]{1,0:T(8,128)(2,1)} %q_hbm.1, bf16[256,512]{1,0:T(8,128)(2,1)} %ck_hbm.1, bf16[256,512]{1,0:T(8,128)(2,1)} %cv_hbm.1, bf16[256,4096]{1,0:T(8,128)(2,1)} %og_hbm.1, s32[1,256]{1,0:T(1,128)} %seg_hbm.1, bf16[32,512]{1,0:T(8,128)(2,1)} %kk_hbm.1, bf16[32,512]{1,0:T(8,128)(2,1)} %kv_hbm.1), custom_call_target="tpu_custom_call" | custom-call | tf_op jit(solution)/shard_map/pallas_call | solution.py:370
  35.3 1.5 %slice_bitcast_fusion = (f32[32,512]{1,0:T(8,128)}, f32[32,512]{1,0:T(8,128)}) fusion(f32[2,32,512]{2,1,0:T(8,128)} %shard_map.86), kind=kLoop, calls=%fused_computation | loop fusion | flops 16384 | bytes 262144 | tf_op jit(solution)/shard_map/squeeze | solution.py:380

commit v4 on v3

--- a/solution.py
+++ b/solution.py
@@ -135,111 +135,119 @@
     def head_cols(g, j):
         return pl.ds(pl.multiple_of(g * width + j * HD, HD), HD)
 
-    def conv_products(g, j, slot):
-        cols, own = head_cols(g, j), pl.ds(pl.multiple_of(g * HD, HD), HD)
-        q, og = q_s[:, cols], og_s[:, cols]
-        s0 = dot_nt(ck_s[:mid, own], q) + bias[:mid, :]
-        s1 = dot_nt(ck_s[mid:, own], q[mid:]) + bias[mid:, mid:]
-        score[slot][:mid, :] = s0
-        score[slot][mid:tokens, mid:] = s1
-        dprob[slot][:mid, :] = dot_nt(cv_s[:mid, own], og)
-        dprob[slot][mid:tokens, mid:] = dot_nt(cv_s[mid:, own], og[mid:])
-        top0 = jnp.max(fold(s0, jnp.max), axis=0, keepdims=True)
-        top1 = jnp.max(fold(s1, jnp.max), axis=0, keepdims=True)
-        tops[slot][0:1, :] = jnp.concatenate(
-            [top0[:, :mid], jnp.maximum(top0[:, mid:], top1)], axis=1
-        ) * factor
-
-    def conv_sums(g, j, slot):
-        top = tops[slot][0:1, :]
-        total = weighted = None
-        for low in range(0, mid, strip):
-            e = jnp.exp2(score[slot][low : low + strip, :] * factor - top)
-            w = e * dprob[slot][low : low + strip, :]
-            e, w = fold(e, jnp.sum), fold(w, jnp.sum)
-            total, weighted = (e, w) if total is None else (total + e, weighted + w)
-        late_total = late_weighted = None
-        for low in range(mid, tokens, strip):
-            e = jnp.exp2(score[slot][low : low + strip, mid:] * factor - top[:, mid:])
-            w = e * dprob[slot][low : low + strip, mid:]
-            e, w = fold(e, jnp.sum), fold(w, jnp.sum)
-            late_total, late_weighted = (
-                (e, w) if late_total is None else (late_total + e, late_weighted + w)
-            )
-
-        def whole(early, late):
-            both = jnp.concatenate([early[:, :mid], early[:, mid:] + late], axis=1)
-            return jnp.sum(both, axis=0, keepdims=True)
-
-        h = g * heads + j
-        stats[h, 0:1, :] = top
-        stats[h, 1:2, :] = whole(total, late_total)
-        stats[h, 2:3, :] = whole(weighted, late_weighted)
-
-    per = heads // 2
-
-    def next_of(step, j):
-        head = jnp.minimum(step * per + j + 1, groups * heads - 1)
+    pairs = groups * heads // 2
+
+    def place_of(pair):
+        head = jnp.clip(pair, 0, pairs - 1) * 2
         return head // heads, lax.rem(head, heads)
 
+    def conv_products(pair, slot):
+        g, j = place_of(pair)
+        own = pl.ds(pl.multiple_of(g * HD, HD), HD)
+        for u in range(2):
+            q, og = q_s[:, head_cols(g, j + u)], og_s[:, head_cols(g, j + u)]
+            s0 = dot_nt(ck_s[:mid, own], q) + bias[:mid, :]
+            s1 = dot_nt(ck_s[mid:, own], q[mid:]) + bias[mid:, mid:]
+            score[slot][u, :mid, :] = s0
+            score[slot][u, mid:tokens, mid:] = s1
+            dprob[slot][u, :mid, :] = dot_nt(cv_s[:mid, own], og)
+            dprob[slot][u, mid:tokens, mid:] = dot_nt(cv_s[mid:, own], og[mid:])
+            top0, top1 = fold(s0, jnp.max), fold(s1, jnp.max)
+            top = jnp.concatenate([top0[:, :mid], jnp.maximum(top0[:, mid:], top1)], axis=1)
+            tops[slot][u : u + 1, :] = jnp.max(top, axis=0, keepdims=True) * factor
+
+    def conv_sums(pair, slot):
+        for u in range(2):
+            top = tops[slot][u : u + 1, :]
+            total = weighted = None
+            for low in range(0, mid, strip):
+                e = jnp.exp2(score[slot][u, low : low + strip, :] * factor - top)
+                w = e * dprob[slot][u, low : low + strip, :]
+                e, w = fold(e, jnp.sum), fold(w, jnp.sum)
+                total, weighted = (e, w) if total is None else (total + e, weighted + w)
+            late_total = late_weighted = None
+            for low in range(mid, tokens, strip):
+                e = jnp.exp2(score[slot][u, low : low + strip, mid:] * factor - top[:, mid:])
+                w = e * dprob[slot][u, low : low + strip, mid:]
+                e, w = fold(e, jnp.sum), fold(w, jnp.sum)
+                late_total, late_weighted = (
+                    (e, w) if late_total is None else (late_total + e, late_weighted + w)
+                )
+
+            def whole(early, late):
+                both = jnp.concatenate([early[:, :mid], early[:, mid:] + late], axis=1)
+                return jnp.sum(both, axis=0, keepdims=True)
+
+            stats[2 * pair + u, 0:1, :] = top
+            stats[2 * pair + u, 1:2, :] = whole(total, late_total)
+            stats[2 * pair + u, 2:3, :] = whole(weighted, late_weighted)
+
     def conv_step(step):
-        g, first = step // 2, lax.rem(step, 2) * per
-
-        @pl.when((first > 0) & (g + 1 < groups))
+        g, late = step // 2, lax.rem(step, 2) == 1
+
+        @pl.when(late & (g + 1 < groups))
         def _():
             for copy in in_copies(g + 1):
                 copy.wait()
 
-        for j in range(per):
-            conv_products(*next_of(step, j), (j + 1) % 2)
-            conv_sums(g, first + j, j % 2)
-
-        @pl.when((first > 0) & (g >= 1))
+        for i in range(per):
+            conv_products(step * per + i + 1, (i + 1) % 2)
+            conv_sums(step * per + i, i % 2)
+
+        @pl.when(late & (g >= 1))
         def _():
             pass_on(g - 1)
 
+    per = heads // 4
     for copy in in_copies(0):
         copy.wait()
-    conv_products(0, 0, 0)
+    conv_products(0, 0)
     pl.loop(0, 2 * groups)(conv_step)
     pass_on(groups - 1)
 
-    def cart_products(g, j, slot):
-        cols = head_cols(g, j)
-        s = dot_nt(buf[g, :, 0].reshape(cart, HD), q_s[:, cols])
-        score[slot][:cart, :] = s
-        tops[slot][0:1, :] = jnp.max(fold(s, jnp.max), axis=0, keepdims=True) * factor
-        dprob[slot][:cart, :] = dot_nt(buf[g, :, 1].reshape(cart, HD), og_s[:, cols])
-
-    def cart_probs(g, j, slot):
-        h = g * heads + j
-        top_conv = stats[h, 0:1, :]
-        top = jnp.maximum(tops[slot][0:1, :], top_conv)
-        total = weighted = None
-        for low in range(0, cart, strip):
-            e = jnp.exp2(score[slot][low : low + strip, :] * factor - top)
-            score[slot][low : low + strip, :] = e
-            w = e * dprob[slot][low : low + strip, :]
-            e, w = fold(e, jnp.sum), fold(w, jnp.sum)
-            total, weighted = (e, w) if total is None else (total + e, weighted + w)
-        shrink = jnp.exp2(top_conv - top)
-        total = stats[h, 1:2, :] * shrink + jnp.sum(total, axis=0, keepdims=True)
-        weighted = stats[h, 2:3, :] * shrink + jnp.sum(weighted, axis=0, keepdims=True)
-        inverse = 1.0 / total
-        delta = weighted * inverse
-        for low in range(0, cart, strip):
-            p = score[slot][low : low + strip, :] * inverse
-            probs[slot][low : low + strip, :] = p.astype(jnp.bfloat16)
-            ds = p * (dprob[slot][low : low + strip, :] - delta)
-            dscore[slot][low : low + strip, :] = ds.astype(jnp.bfloat16)
-
-    def cart_grads(g, j, slot):
-        cols = head_cols(g, j)
+    def cart_products(pair, slot):
+        g, j = place_of(pair)
+        for u in range(2):
+            cols = head_cols(g, j + u)
+            s = dot_nt(buf[g, :, 0].reshape(cart, HD), q_s[:, cols])
+            score[slot][u, :cart, :] = s
+            tops[slot][u : u + 1, :] = jnp.max(fold(s, jnp.max), axis=0, keepdims=True) * factor
+            dprob[slot][u, :cart, :] = dot_nt(buf[g, :, 1].reshape(cart, HD), og_s[:, cols])
+
+    def cart_probs(pair, slot):
+        for u in range(2):
+            h = 2 * pair + u
+            top_conv = stats[h, 0:1, :]
+            top = jnp.maximum(tops[slot][u : u + 1, :], top_conv)
+            total = weighted = None
+            for low in range(0, cart, strip):
+                e = jnp.exp2(score[slot][u, low : low + strip, :] * factor - top)
+                score[slot][u, low : low + strip, :] = e
+                w = e * dprob[slot][u, low : low + strip, :]
+                e, w = fold(e, jnp.sum), fold(w, jnp.sum)
+                total, weighted = (e, w) if total is None else (total + e, weighted + w)
+            shrink = jnp.exp2(top_conv - top)
+            total = stats[h, 1:2, :] * shrink + jnp.sum(total, axis=0, keepdims=True)
+            weighted = stats[h, 2:3, :] * shrink + jnp.sum(weighted, axis=0, keepdims=True)
+            inverse = 1.0 / total
+            delta = weighted * inverse
+            cols = slice(u * tokens, (u + 1) * tokens)
+            for low in range(0, cart, strip):
+                p = score[slot][u, low : low + strip, :] * inverse
+                probs[slot][low : low + strip, cols] = p.astype(jnp.bfloat16)
+                ds = p * (dprob[slot][u, low : low + strip, :] - delta)
+                dscore[slot][low : low + strip, cols] = ds.astype(jnp.bfloat16)
+
+    def cart_grads(pair, slot):
+        g, j = place_of(pair)
         for kind, (left, right) in enumerate(((dscore, q_s), (probs, og_s))):
-            term = dot(left[slot][...], right[:, cols]).reshape(half, 2, rows, HD)
+            both = jnp.concatenate([right[:, head_cols(g, j + u)] for u in range(2)], axis=0)
+            term = dot(left[slot][...], both).reshape(half, 2, rows, HD)
             part[g, :, :, kind] += term
 
     part[...] = jnp.zeros_like(part)
+    for ref in (probs_b, dscore_b):
+        ref[...] = jnp.zeros_like(ref)
     peers = [lax.rem(me + 2 * i, n) for i in range(half)]
     def pair_copy(g):
         return remote(
@@ -282,32 +290,34 @@
         out_ref[:, :, g * HD : (g + 1) * HD] = total
 
     def cart_step(step):
-        g, first = step // 2, lax.rem(step, 2) * per
-
-        @pl.when((first > 0) & (g + 1 < groups))
+        g, late = step // 2, lax.rem(step, 2) == 1
+
+        @pl.when(late & (g + 1 < groups))
         def _():
             gathered(g + 1)
 
-        for j in range(per):
-            cart_products(*next_of(step, j), (j + 1) % 2)
-            cart_probs(g, first + j, j % 2)
-            cart_grads(g, first + j, j % 2)
-
-        @pl.when(first > 0)
-        def _():
-            pair_copy(g).start()
-
-        @pl.when((first == 0) & (g >= 1))
+        for i in range(per):
+            cart_grads(step * per + i - 1, (i + 1) % 2)
+            cart_products(step * per + i + 1, (i + 1) % 2)
+            cart_probs(step * per + i, i % 2)
+
+        @pl.when(jnp.logical_not(late) & (g >= 1))
+        def _():
+            pair_copy(g - 1).start()
+
+        @pl.when(late & (g >= 1))
         def _():
             start_place(g - 1)
 
-        @pl.when((first == 0) & (g >= 2))
+        @pl.when(jnp.logical_not(late) & (g >= 2))
         def _():
             start_all(g - 2)
 
     gathered(0)
-    cart_products(0, 0, 0)
+    cart_products(0, 0)
     pl.loop(0, 2 * groups)(cart_step)
+    cart_grads(pairs - 1, 1)
+    pair_copy(groups - 1).start()
     start_place(groups - 1)
     if groups > 1:
         start_all(groups - 2)
@@ -353,9 +363,9 @@
             pltpu.VMEM((groups, half, 2, rows, HD), bf16),
             pltpu.VMEM((groups, half, 2, rows, HD), bf16),
             pltpu.VMEM((groups, nd, 2, rows, HD), bf16),
-            *[pltpu.VMEM((max(n * rows, tokens), tokens), f32)] * 4,
+            *[pltpu.VMEM((2, max(n * rows, tokens), tokens), f32)] * 4,
             *[pltpu.VMEM((8, tokens), f32)] * 2,
-            *[pltpu.VMEM((n * rows, tokens), bf16)] * 4,
+            *[pltpu.VMEM((n * rows, 2 * tokens), bf16)] * 4,
             dma((2, groups)),
             dma((3,)),
             dma((2, groups)),

time: 37 us -> 41.9 us (1.13)
  Pallas kernels: 34.7 us -> 39.5 us
    pallas_call x1, Pallas kernels: 34.7 us -> 39.5 us  [per_device(): pl.pallas_call(functools.partial(kernel, n, nd, groups, heads), out_shape...]
where the time goes in v4:
time: 41.9 us; the launch traced here: 41.7 us
  Pallas kernels  39.5 us (94%)
  other arithmetic  1.53 us (4%)
  between operations  0.64 us (2%)
    pallas_call x1, Pallas kernels, per_device(): pl.pallas_call(functools.partial(kernel, n, nd, groups, heads), out_shape...  39.5 us
    squeeze x1, other arithmetic, per_device(): return (out[0] * (1.0 / math.sqrt(HD)), out[1])  1.53 us

profile of v4, /device:TPU:0, one launch (start us, length us, event | category | flops | bytes accessed | tf_op | source)
XLA Modules:
  0.0 41.7 jit_solution(2095961042307804925)
XLA Ops:
  0.6 39.5 %shard_map.86 = f32[2,32,512]{2,1,0:T(8,128)} custom-call(bf16[256,4096]{1,0:T(8,128)(2,1)} %q_hbm.1, bf16[256,512]{1,0:T(8,128)(2,1)} %ck_hbm.1, bf16[256,512]{1,0:T(8,128)(2,1)} %cv_hbm.1, bf16[256,4096]{1,0:T(8,128)(2,1)} %og_hbm.1, s32[1,256]{1,0:T(1,128)} %seg_hbm.1, bf16[32,512]{1,0:T(8,128)(2,1)} %kk_hbm.1, bf16[32,512]{1,0:T(8,128)(2,1)} %kv_hbm.1), custom_call_target="tpu_custom_call" | custom-call | tf_op jit(solution)/shard_map/pallas_call | solution.py:380
  40.2 1.5 %slice_bitcast_fusion = (f32[32,512]{1,0:T(8,128)}, f32[32,512]{1,0:T(8,128)}) fusion(f32[2,32,512]{2,1,0:T(8,128)} %shard_map.86), kind=kLoop, calls=%fused_computation | loop fusion | flops 16384 | bytes 262144 | tf_op jit(solution)/shard_map/squeeze | solution.py:390

commit v5 on v3

--- a/solution.py
+++ b/solution.py
@@ -10,11 +10,6 @@
 
 HD = 128
 MESH = pl.DeviceIdType.MESH
-NT = (((1,), (1,)), ((), ()))
-
-
-def dot_nt(a, b):
-    return lax.dot_general(a, b, NT, preferred_element_type=jnp.float32)
 
 
 def dot(a, b):
@@ -25,7 +20,7 @@
     n, nd, groups, heads,
     q_hbm, ck_hbm, cv_hbm, og_hbm, seg_hbm, kk_hbm, kv_hbm,
     out_ref,
-    q_s, og_s, ck_s, cv_s, seg_s, bias, stats, buf, part, r1, s2, r2, r3,
+    q_s, og_s, q_t, og_t, ck_s, cv_s, seg_s, bias, stats, buf, part, r1, s2, r2, r3,
     score_a, score_b, dprob_a, dprob_b, tops_a, tops_b, probs_a, probs_b, dscore_a, dscore_b,
     in_sem, conv_sem, cart_sem,
     g_send, g_recv, f_send, f_recv, s1_send, s1_recv, s2_send, s2_recv, s3_send, s3_recv,
@@ -137,13 +132,15 @@
 
     def conv_products(g, j, slot):
         cols, own = head_cols(g, j), pl.ds(pl.multiple_of(g * HD, HD), HD)
-        q, og = q_s[:, cols], og_s[:, cols]
-        s0 = dot_nt(ck_s[:mid, own], q) + bias[:mid, :]
-        s1 = dot_nt(ck_s[mid:, own], q[mid:]) + bias[mid:, mid:]
+        h = g * heads + j
+        q, og = q_s[:, cols].T, og_s[:, cols].T
+        q_t[h], og_t[h] = q, og
+        s0 = dot(ck_s[:mid, own], q) + bias[:mid, :]
+        s1 = dot(ck_s[mid:, own], q[:, mid:]) + bias[mid:, mid:]
         score[slot][:mid, :] = s0
         score[slot][mid:tokens, mid:] = s1
-        dprob[slot][:mid, :] = dot_nt(cv_s[:mid, own], og)
-        dprob[slot][mid:tokens, mid:] = dot_nt(cv_s[mid:, own], og[mid:])
+        dprob[slot][:mid, :] = dot(cv_s[:mid, own], og)
+        dprob[slot][mid:tokens, mid:] = dot(cv_s[mid:, own], og[:, mid:])
         top0 = jnp.max(fold(s0, jnp.max), axis=0, keepdims=True)
         top1 = jnp.max(fold(s1, jnp.max), axis=0, keepdims=True)
         tops[slot][0:1, :] = jnp.concatenate(
@@ -205,11 +202,11 @@
     pass_on(groups - 1)
 
     def cart_products(g, j, slot):
-        cols = head_cols(g, j)
-        s = dot_nt(buf[g, :, 0].reshape(cart, HD), q_s[:, cols])
+        h = g * heads + j
+        s = dot(buf[g, :, 0].reshape(cart, HD), q_t[h])
         score[slot][:cart, :] = s
         tops[slot][0:1, :] = jnp.max(fold(s, jnp.max), axis=0, keepdims=True) * factor
-        dprob[slot][:cart, :] = dot_nt(buf[g, :, 1].reshape(cart, HD), og_s[:, cols])
+        dprob[slot][:cart, :] = dot(buf[g, :, 1].reshape(cart, HD), og_t[h])
 
     def cart_probs(g, j, slot):
         h = g * heads + j
@@ -342,6 +339,7 @@
         scratch = [
             pltpu.VMEM(queries.shape, bf16),
             pltpu.VMEM(out_grad.shape, bf16),
+            *[pltpu.VMEM((groups * heads, HD, tokens), bf16)] * 2,
             pltpu.VMEM(conv_keys.shape, bf16),
             pltpu.VMEM(conv_values.shape, bf16),
             pltpu.VMEM(segment_ids.shape, jnp.int32),

time: 37 us -> 36.9 us (level)
  no operation moved by 1% of the time
where the time goes in v5:
time: 36.9 us; the launch traced here: 36.8 us
  Pallas kernels  34.6 us (94%)
  other arithmetic  1.53 us (4%)
  between operations  0.64 us (2%)
    pallas_call x1, Pallas kernels, per_device(): pl.pallas_call(functools.partial(kernel, n, nd, groups, heads), out_shape...  34.6 us
    squeeze x1, other arithmetic, per_device(): return (out[0] * (1.0 / math.sqrt(HD)), out[1])  1.53 us

profile of v5, /device:TPU:0, one launch (start us, length us, event | category | flops | bytes accessed | tf_op | source)
XLA Modules:
  0.0 36.8 jit_solution(8234166279821166937)
XLA Ops:
  0.6 34.6 %shard_map.86 = f32[2,32,512]{2,1,0:T(8,128)} custom-call(bf16[256,4096]{1,0:T(8,128)(2,1)} %q_hbm.1, bf16[256,512]{1,0:T(8,128)(2,1)} %ck_hbm.1, bf16[256,512]{1,0:T(8,128)(2,1)} %cv_hbm.1, bf16[256,4096]{1,0:T(8,128)(2,1)} %og_hbm.1, s32[1,256]{1,0:T(1,128)} %seg_hbm.1, bf16[32,512]{1,0:T(8,128)(2,1)} %kk_hbm.1, bf16[32,512]{1,0:T(8,128)(2,1)} %kv_hbm.1), custom_call_target="tpu_custom_call" | custom-call | tf_op jit(solution)/shard_map/pallas_call | solution.py:368
  35.2 1.5 %slice_bitcast_fusion = (f32[32,512]{1,0:T(8,128)}, f32[32,512]{1,0:T(8,128)}) fusion(f32[2,32,512]{2,1,0:T(8,128)} %shard_map.86), kind=kLoop, calls=%fused_computation | loop fusion | flops 16384 | bytes 262144 | tf_op jit(solution)/shard_map/squeeze | solution.py:378

commit v6 on v3

--- a/solution.py
+++ b/solution.py
@@ -25,7 +25,7 @@
     n, nd, groups, heads,
     q_hbm, ck_hbm, cv_hbm, og_hbm, seg_hbm, kk_hbm, kv_hbm,
     out_ref,
-    q_s, og_s, ck_s, cv_s, seg_s, bias, stats, buf, part, r1, s2, r2, r3,
+    q_s, og_s, ck_s, cv_s, seg_s, bias, buf, part, r1, s2, r2, r3,
     score_a, score_b, dprob_a, dprob_b, tops_a, tops_b, probs_a, probs_b, dscore_a, dscore_b,
     in_sem, conv_sem, cart_sem,
     g_send, g_recv, f_send, f_recv, s1_send, s1_recv, s2_send, s2_recv, s3_send, s3_recv,
@@ -135,103 +135,54 @@
     def head_cols(g, j):
         return pl.ds(pl.multiple_of(g * width + j * HD, HD), HD)
 
-    def conv_products(g, j, slot):
+    def products(g, j, slot):
         cols, own = head_cols(g, j), pl.ds(pl.multiple_of(g * HD, HD), HD)
-        q, og = q_s[:, cols], og_s[:, cols]
-        s0 = dot_nt(ck_s[:mid, own], q) + bias[:mid, :]
-        s1 = dot_nt(ck_s[mid:, own], q[mid:]) + bias[mid:, mid:]
-        score[slot][:mid, :] = s0
-        score[slot][mid:tokens, mid:] = s1
-        dprob[slot][:mid, :] = dot_nt(cv_s[:mid, own], og)
-        dprob[slot][mid:tokens, mid:] = dot_nt(cv_s[mid:, own], og[mid:])
-        top0 = jnp.max(fold(s0, jnp.max), axis=0, keepdims=True)
-        top1 = jnp.max(fold(s1, jnp.max), axis=0, keepdims=True)
-        tops[slot][0:1, :] = jnp.concatenate(
-            [top0[:, :mid], jnp.maximum(top0[:, mid:], top1)], axis=1
-        ) * factor
-
-    def conv_sums(g, j, slot):
+        keys = jnp.concatenate([buf[g, :, 0].reshape(cart, HD), ck_s[:, own]], axis=0)
+        values = jnp.concatenate([buf[g, :, 1].reshape(cart, HD), cv_s[:, own]], axis=0)
+        s = dot_nt(keys, q_s[:, cols])
+        conv = s[cart:] + bias[...]
+        score[slot][:cart, :] = s[:cart]
+        score[slot][cart:, :] = conv
+        top = jnp.maximum(fold(s[:cart], jnp.max), fold(conv, jnp.max))
+        tops[slot][0:1, :] = jnp.max(top, axis=0, keepdims=True) * factor
+        dprob[slot][...] = dot_nt(values, og_s[:, cols])
+
+    def softmax(slot):
         top = tops[slot][0:1, :]
-        total = weighted = None
-        for low in range(0, mid, strip):
-            e = jnp.exp2(score[slot][low : low + strip, :] * factor - top)
-            w = e * dprob[slot][low : low + strip, :]
-            e, w = fold(e, jnp.sum), fold(w, jnp.sum)
-            total, weighted = (e, w) if total is None else (total + e, weighted + w)
-        late_total = late_weighted = None
-        for low in range(mid, tokens, strip):
-            e = jnp.exp2(score[slot][low : low + strip, mid:] * factor - top[:, mid:])
-            w = e * dprob[slot][low : low + strip, mid:]
-            e, w = fold(e, jnp.sum), fold(w, jnp.sum)
-            late_total, late_weighted = (
-                (e, w) if late_total is None else (late_total + e, late_weighted + w)
-            )
+
+        def sums(low, lanes):
+            e = jnp.exp2(score[slot][low : low + strip, lanes] * factor - top[:, lanes])
+            w = e * dprob[slot][low : low + strip, lanes]
+            return e, fold(e, jnp.sum), fold(w, jnp.sum)
+
+        total = weighted = 0.0
+        for low in range(0, cart + mid, strip):
+            e, e_sum, w_sum = sums(low, slice(0, tokens))
+            if low < cart:
+                score[slot][low : low + strip, :] = e
+            total, weighted = total + e_sum, weighted + w_sum
+        late_total = late_weighted = 0.0
+        for low in range(cart + mid, cart + tokens, strip):
+            _, e_sum, w_sum = sums(low, slice(mid, tokens))
+            late_total, late_weighted = late_total + e_sum, late_weighted + w_sum
 
         def whole(early, late):
             both = jnp.concatenate([early[:, :mid], early[:, mid:] + late], axis=1)
             return jnp.sum(both, axis=0, keepdims=True)
 
-        h = g * heads + j
-        stats[h, 0:1, :] = top
-        stats[h, 1:2, :] = whole(total, late_total)
-        stats[h, 2:3, :] = whole(weighted, late_weighted)
-
-    per = heads // 2
-
-    def next_of(step, j):
-        head = jnp.minimum(step * per + j + 1, groups * heads - 1)
-        return head // heads, lax.rem(head, heads)
-
-    def conv_step(step):
-        g, first = step // 2, lax.rem(step, 2) * per
-
-        @pl.when((first > 0) & (g + 1 < groups))
-        def _():
-            for copy in in_copies(g + 1):
-                copy.wait()
-
-        for j in range(per):
-            conv_products(*next_of(step, j), (j + 1) % 2)
-            conv_sums(g, first + j, j % 2)
-
-        @pl.when((first > 0) & (g >= 1))
-        def _():
-            pass_on(g - 1)
-
-    for copy in in_copies(0):
-        copy.wait()
-    conv_products(0, 0, 0)
-    pl.loop(0, 2 * groups)(conv_step)
-    pass_on(groups - 1)
-
-    def cart_products(g, j, slot):
-        cols = head_cols(g, j)
-        s = dot_nt(buf[g, :, 0].reshape(cart, HD), q_s[:, cols])
-        score[slot][:cart, :] = s
-        tops[slot][0:1, :] = jnp.max(fold(s, jnp.max), axis=0, keepdims=True) * factor
-        dprob[slot][:cart, :] = dot_nt(buf[g, :, 1].reshape(cart, HD), og_s[:, cols])
-
-    def cart_probs(g, j, slot):
-        h = g * heads + j
-        top_conv = stats[h, 0:1, :]
-        top = jnp.maximum(tops[slot][0:1, :], top_conv)
-        total = weighted = None
-        for low in range(0, cart, strip):
-            e = jnp.exp2(score[slot][low : low + strip, :] * factor - top)
-            score[slot][low : low + strip, :] = e
-            w = e * dprob[slot][low : low + strip, :]
-            e, w = fold(e, jnp.sum), fold(w, jnp.sum)
-            total, weighted = (e, w) if total is None else (total + e, weighted + w)
-        shrink = jnp.exp2(top_conv - top)
-        total = stats[h, 1:2, :] * shrink + jnp.sum(total, axis=0, keepdims=True)
-        weighted = stats[h, 2:3, :] * shrink + jnp.sum(weighted, axis=0, keepdims=True)
-        inverse = 1.0 / total
-        delta = weighted * inverse
+        inverse = 1.0 / whole(total, late_total)
+        delta = whole(weighted, late_weighted) * inverse
         for low in range(0, cart, strip):
             p = score[slot][low : low + strip, :] * inverse
             probs[slot][low : low + strip, :] = p.astype(jnp.bfloat16)
             ds = p * (dprob[slot][low : low + strip, :] - delta)
             dscore[slot][low : low + strip, :] = ds.astype(jnp.bfloat16)
+
+    per = heads // 2
+
+    def next_of(step, j):
+        head = jnp.minimum(step * per + j + 1, groups * heads - 1)
+        return head // heads, lax.rem(head, heads)
 
     def cart_grads(g, j, slot):
         cols = head_cols(g, j)
@@ -281,16 +232,22 @@
             total = total + r3[g, i].astype(jnp.float32)
         out_ref[:, :, g * HD : (g + 1) * HD] = total
 
-    def cart_step(step):
+    def step_body(step):
         g, first = step // 2, lax.rem(step, 2) * per
 
+        @pl.when((first == 0) & (g + 1 < groups))
+        def _():
+            pass_on(g + 1)
+
         @pl.when((first > 0) & (g + 1 < groups))
         def _():
+            for copy in in_copies(g + 1):
+                copy.wait()
             gathered(g + 1)
 
         for j in range(per):
-            cart_products(*next_of(step, j), (j + 1) % 2)
-            cart_probs(g, first + j, j % 2)
+            products(*next_of(step, j), (j + 1) % 2)
+            softmax(j % 2)
             cart_grads(g, first + j, j % 2)
 
         @pl.when(first > 0)
@@ -305,9 +262,12 @@
         def _():
             start_all(g - 2)
 
+    pass_on(0)
+    for copy in in_copies(0):
+        copy.wait()
     gathered(0)
-    cart_products(0, 0, 0)
-    pl.loop(0, 2 * groups)(cart_step)
+    products(0, 0, 0)
+    pl.loop(0, 2 * groups)(step_body)
     start_place(groups - 1)
     if groups > 1:
         start_all(groups - 2)
@@ -346,14 +306,13 @@
             pltpu.VMEM(conv_values.shape, bf16),
             pltpu.VMEM(segment_ids.shape, jnp.int32),
             pltpu.VMEM((tokens, tokens), f32),
-            pltpu.VMEM((groups * heads, 8, tokens), f32),
             pltpu.VMEM((groups, n, 2, rows, HD), bf16),
             pltpu.VMEM((groups, half, 2, 2, rows, HD), f32),
             pltpu.VMEM((groups, half, 2, rows, HD), f32),
             pltpu.VMEM((groups, half, 2, rows, HD), bf16),
             pltpu.VMEM((groups, half, 2, rows, HD), bf16),
             pltpu.VMEM((groups, nd, 2, rows, HD), bf16),
-            *[pltpu.VMEM((max(n * rows, tokens), tokens), f32)] * 4,
+            *[pltpu.VMEM((n * rows + tokens, tokens), f32)] * 4,
             *[pltpu.VMEM((8, tokens), f32)] * 2,
             *[pltpu.VMEM((n * rows, tokens), bf16)] * 4,
             dma((2, groups)),

time: 37 us -> 37.9 us (1.024)
  Pallas kernels: 34.7 us -> 35.5 us
    pallas_call x1, Pallas kernels: 34.7 us -> 35.5 us  [per_device(): pl.pallas_call(functools.partial(kernel, n, nd, groups, heads), out_shape...]
where the time goes in v6:
time: 37.9 us; the launch traced here: 37.7 us
  Pallas kernels  35.5 us (94%)
  other arithmetic  1.53 us (4%)
  between operations  0.64 us (2%)
    pallas_call x1, Pallas kernels, per_device(): pl.pallas_call(functools.partial(kernel, n, nd, groups, heads), out_shape...  35.5 us
    squeeze x1, other arithmetic, per_device(): return (out[0] * (1.0 / math.sqrt(HD)), out[1])  1.53 us

profile of v6, /device:TPU:0, one launch (start us, length us, event | category | flops | bytes accessed | tf_op | source)
XLA Modules:
  0.0 37.7 jit_solution(12457804696922188698)
XLA Ops:
  0.6 35.5 %shard_map.86 = f32[2,32,512]{2,1,0:T(8,128)} custom-call(bf16[256,4096]{1,0:T(8,128)(2,1)} %q_hbm.1, bf16[256,512]{1,0:T(8,128)(2,1)} %ck_hbm.1, bf16[256,512]{1,0:T(8,128)(2,1)} %cv_hbm.1, bf16[256,4096]{1,0:T(8,128)(2,1)} %og_hbm.1, s32[1,256]{1,0:T(1,128)} %seg_hbm.1, bf16[32,512]{1,0:T(8,128)(2,1)} %kk_hbm.1, bf16[32,512]{1,0:T(8,128)(2,1)} %kv_hbm.1), custom_call_target="tpu_custom_call" | custom-call | tf_op jit(solution)/shard_map/pallas_call | solution.py:329
  36.2 1.5 %slice_bitcast_fusion = (f32[32,512]{1,0:T(8,128)}, f32[32,512]{1,0:T(8,128)}) fusion(f32[2,32,512]{2,1,0:T(8,128)} %shard_map.86), kind=kLoop, calls=%fused_computation | loop fusion | flops 16384 | bytes 262144 | tf_op jit(solution)/shard_map/squeeze | solution.py:339

commit v7 on v5

--- a/solution.py
+++ b/solution.py
@@ -179,26 +179,24 @@
         head = jnp.minimum(step * per + j + 1, groups * heads - 1)
         return head // heads, lax.rem(head, heads)
 
-    def conv_step(step):
-        g, first = step // 2, lax.rem(step, 2) * per
-
-        @pl.when((first > 0) & (g + 1 < groups))
+    def conv_group(g):
+        @pl.when(g + 1 < groups)
         def _():
             for copy in in_copies(g + 1):
                 copy.wait()
 
-        for j in range(per):
-            conv_products(*next_of(step, j), (j + 1) % 2)
-            conv_sums(g, first + j, j % 2)
-
-        @pl.when((first > 0) & (g >= 1))
+        for j in range(heads):
+            conv_products(*next_of(2 * g, j), (j + 1) % 2)
+            conv_sums(g, j, j % 2)
+
+        @pl.when(g >= 1)
         def _():
             pass_on(g - 1)
 
     for copy in in_copies(0):
         copy.wait()
     conv_products(0, 0, 0)
-    pl.loop(0, 2 * groups)(conv_step)
+    pl.loop(0, groups)(conv_group)
     pass_on(groups - 1)
 
     def cart_products(g, j, slot):
@@ -287,8 +285,10 @@
 
         for j in range(per):
             cart_products(*next_of(step, j), (j + 1) % 2)
+            if j > 0:
+                cart_grads(g, first + j - 1, (j - 1) % 2)
             cart_probs(g, first + j, j % 2)
-            cart_grads(g, first + j, j % 2)
+        cart_grads(g, first + per - 1, (per - 1) % 2)
 
         @pl.when(first > 0)
         def _():

time: 36.9 us -> 36.6 us (level)
  no operation moved by 1% of the time
where the time goes in v7:
time: 36.6 us; the launch traced here: 36.4 us
  Pallas kernels  34.3 us (94%)
  other arithmetic  1.53 us (4%)
  between operations  0.64 us (2%)
    pallas_call x1, Pallas kernels, per_device(): pl.pallas_call(functools.partial(kernel, n, nd, groups, heads), out_shape...  34.3 us
    squeeze x1, other arithmetic, per_device(): return (out[0] * (1.0 / math.sqrt(HD)), out[1])  1.53 us

profile of v7, /device:TPU:0, one launch (start us, length us, event | category | flops | bytes accessed | tf_op | source)
XLA Modules:
  0.0 36.4 jit_solution(16255874199799843490)
XLA Ops:
  0.6 34.3 %shard_map.86 = f32[2,32,512]{2,1,0:T(8,128)} custom-call(bf16[256,4096]{1,0:T(8,128)(2,1)} %q_hbm.1, bf16[256,512]{1,0:T(8,128)(2,1)} %ck_hbm.1, bf16[256,512]{1,0:T(8,128)(2,1)} %cv_hbm.1, bf16[256,4096]{1,0:T(8,128)(2,1)} %og_hbm.1, s32[1,256]{1,0:T(1,128)} %seg_hbm.1, bf16[32,512]{1,0:T(8,128)(2,1)} %kk_hbm.1, bf16[32,512]{1,0:T(8,128)(2,1)} %kv_hbm.1), custom_call_target="tpu_custom_call" | custom-call | tf_op jit(solution)/shard_map/pallas_call | solution.py:368
  34.9 1.5 %slice_bitcast_fusion = (f32[32,512]{1,0:T(8,128)}, f32[32,512]{1,0:T(8,128)}) fusion(f32[2,32,512]{2,1,0:T(8,128)} %shard_map.86), kind=kLoop, calls=%fused_computation | loop fusion | flops 16384 | bytes 262144 | tf_op jit(solution)/shard_map/squeeze | solution.py:378

commit v8 on v5

--- a/solution.py
+++ b/solution.py
@@ -122,7 +122,7 @@
     bias[...] = jnp.where(allowed, 0.0, -1e30)
     mid = tokens // 2
 
-    strip = 32
+    strip = 16
 
     def fold(x, reduce):
         return reduce(x.reshape(x.shape[0] // 8, 8, x.shape[1]), axis=0)

time: 36.9 us -> 36.9 us (level)
  no operation moved by 1% of the time
where the time goes in v8:
time: 36.9 us; the launch traced here: 36.8 us
  Pallas kernels  34.6 us (94%)
  other arithmetic  1.53 us (4%)
  between operations  0.64 us (2%)
    pallas_call x1, Pallas kernels, per_device(): pl.pallas_call(functools.partial(kernel, n, nd, groups, heads), out_shape...  34.6 us
    squeeze x1, other arithmetic, per_device(): return (out[0] * (1.0 / math.sqrt(HD)), out[1])  1.53 us

profile of v8, /device:TPU:0, one launch (start us, length us, event | category | flops | bytes accessed | tf_op | source)
XLA Modules:
  0.0 36.8 jit_solution(13509268564350824014)
XLA Ops:
  0.6 34.6 %shard_map.86 = f32[2,32,512]{2,1,0:T(8,128)} custom-call(bf16[256,4096]{1,0:T(8,128)(2,1)} %q_hbm.1, bf16[256,512]{1,0:T(8,128)(2,1)} %ck_hbm.1, bf16[256,512]{1,0:T(8,128)(2,1)} %cv_hbm.1, bf16[256,4096]{1,0:T(8,128)(2,1)} %og_hbm.1, s32[1,256]{1,0:T(1,128)} %seg_hbm.1, bf16[32,512]{1,0:T(8,128)(2,1)} %kk_hbm.1, bf16[32,512]{1,0:T(8,128)(2,1)} %kv_hbm.1), custom_call_target="tpu_custom_call" | custom-call | tf_op jit(solution)/shard_map/pallas_call | solution.py:368
  35.2 1.5 %slice_bitcast_fusion = (f32[32,512]{1,0:T(8,128)}, f32[32,512]{1,0:T(8,128)}) fusion(f32[2,32,512]{2,1,0:T(8,128)} %shard_map.86), kind=kLoop, calls=%fused_computation | loop fusion | flops 16384 | bytes 262144 | tf_op jit(solution)/shard_map/squeeze | solution.py:378
